TPU v7x, 32 devices: a whole 2x2x4 slice. The times are simulated.
32 devices in a mesh: groups: 2 (over y), wide: 4 (over z), trans: 2 (over x), sub: 2 (over core).
Axes of the slice: x: 2, y: 2, z: 4, core: 2. Of those that a mesh axis runs over, the one named last changes fastest.
Arguments:
- start_vectors: float32 [24, 32, 16, 256], P(None, ('groups', 'wide'), ('trans', 'sub')), parts along dimension 1, may hold values from -6 to 6
- hopping: bfloat16 [9, 256, 256], replicated, may hold values from -0.0625 to 0.0625
- pairing: bfloat16 [5, 256, 256], replicated, may hold values from -0.0625 to 0.0625
- onsite: bfloat16 [3, 256, 256], replicated, may hold values from -0.125 to 0.125
- region: int32 [32, 16], P(('groups', 'wide'), ('trans', 'sub')), parts along dimension 0, may hold values from 0 to 2
Outputs:
- cheb_last: float32 [24, 32, 16, 256], P(None, ('groups', 'wide'), ('trans', 'sub')), parts along dimension 1
- cheb_before: float32 [24, 32, 16, 256], P(None, ('groups', 'wide'), ('trans', 'sub')), parts along dimension 1
There are 2 independent parts, one for each index of `groups`. A program takes and returns all parts, laid end to end along the dimension named above; an argument that names none is the same for every part. Nothing has to cross between parts.
All inputs are finite; a program needn't handle non-finite values.
Results may differ from a plain program's by a relative error of at most 0.0046.
Values may be sent and summed in bfloat16 or wider, within the bound.
A program may use at most 64 MiB of HBM per device.

v0:
```python
import jax
import jax.numpy as jnp
from jax import lax
from jax.sharding import PartitionSpec as P

ITERS = 4


HOP_OFFSETS = [(-1, -1), (-1, 0), (-1, 1), (0, -1), (0, 0), (0, 1), (1, -1), (1, 0), (1, 1)]
PAIR_OFFSETS = [(0, 0), (1, 0), (-1, 0), (0, 1), (0, -1)]


def with_halo(array, sides, width):
    for axis, dim in sides:
        size, length = (lax.axis_size(axis), array.shape[dim])
        up = [(i, (i + 1) % size) for i in range(size - 1)]
        down = [(j, i) for i, j in up]
        last = lax.slice_in_dim(array, length - width, length, axis=dim)
        leading = lax.slice_in_dim(array, 0, width, axis=dim)
        before = lax.ppermute(last, axis, up)
        after = lax.ppermute(leading, axis, down)
        array = jnp.concatenate([before, array, after], axis=dim)
    return array


def swapped(value, axis, bit):
    mask = 2**bit
    pairs = [(source, source ^ mask) for source in range(lax.axis_size(axis))]
    return lax.ppermute(value, axis, pairs)


def block_product(slab, matrix):
    return jnp.einsum("vxyb,bc->vxyc", slab, matrix, preferred_element_type=jnp.float32)


def shards(start_vectors, hopping, pairing, onsite, region):
    vectors, count_x, count_y, orbitals = start_vectors.shape
    wide_index = lax.axis_index("wide")
    wide_count = lax.axis_size("wide")
    half_size = wide_count // 2
    bit_count = wide_count.bit_length() - 1
    electron = wide_index < half_size
    sector_sign = jnp.where(electron, 1, -1).astype(jnp.int32)
    sector_scale = jnp.where(electron, 1.0, -1.0).astype(jnp.float32)
    pair_used = jnp.where(electron, pairing, jnp.swapaxes(pairing, 1, 2))
    kinds = jnp.arange(onsite.shape[0], dtype=jnp.int32)
    chosen = (region[None, :, :] == kinds[:, None, None]).astype(jnp.bfloat16)
    onsite_blocks = jnp.sum(chosen[:, :, :, None, None] * onsite[:, None, None, :, :], axis=0)
    anchor = jnp.int32(0)

    def window(padded, start_x, start_y):
        starts = (anchor, jnp.asarray(start_x, jnp.int32), jnp.asarray(start_y, jnp.int32), anchor)
        return lax.dynamic_slice(padded, starts, (vectors, count_x, count_y, orbitals))

    def apply_hamiltonian(rounded):
        padded = with_halo(rounded, (("wide", 1), (("trans", "sub"), 2)), 1)
        received = padded
        for bit_index in range(bit_count):
            received = swapped(received, "wide", bit_index)
        partner = jnp.flip(received, 1)
        normal = jnp.einsum(
            "vxyb,xybc->vxyc", rounded, onsite_blocks, preferred_element_type=jnp.float32
        )
        for offset_index, (shift_x, shift_y) in enumerate(HOP_OFFSETS):
            slab = window(padded, 1 + sector_sign * shift_x, 1 + shift_y)
            normal = normal + block_product(slab, hopping[offset_index])
        paired = jnp.zeros(rounded.shape, jnp.float32)
        for offset_index, (shift_x, shift_y) in enumerate(PAIR_OFFSETS):
            slab = window(partner, 1 + shift_x, 1 + sector_sign * shift_y)
            paired = paired + block_product(slab, pair_used[offset_index])
        return sector_scale * normal + paired

    previous = start_vectors
    current = apply_hamiltonian(start_vectors.astype(jnp.bfloat16))
    for step in range(ITERS - 1):
        following = 2.0 * apply_hamiltonian(current.astype(jnp.bfloat16)) - previous
        previous = current
        current = following
    return (current, previous)


def solution(mesh):
    in_specs = (
        P(None, ("groups", "wide"), ("trans", "sub"), None),
        P(),
        P(),
        P(),
        P(("groups", "wide"), ("trans", "sub")),
    )
    out_specs = (
        P(None, ("groups", "wide"), ("trans", "sub"), None),
        P(None, ("groups", "wide"), ("trans", "sub"), None),
    )
    return jax.shard_map(shards, mesh=mesh, in_specs=in_specs, out_specs=out_specs, check_vma=False)
```

profile of v0, /device:TPU:0, one launch (start us, length us, event | category | flops | bytes accessed | tf_op | source)
XLA Modules:
  0.0 257.7 jit_solution(4617515354599853103)
XLA Ops:
  1.9 4.9 %collective-permute-start = (bf16[24,1,4,256]{3,0,2,1:T(8,128)(2,1)S(1)}, bf16[24,1,4,256]{3,0,2,1:T(8,128)(2,1)S(1)}, u32[]{:S(2)}, u32[]{:S(2)}) collective-permute-start(bf16[24,1,4,256]{3,0,2,1:T(8,128)(2,1)S(1)} %get-tuple-element.32), channel_id=1, source_target_pairs={{0,4},{4,8},{8,12},{1,5},{5,9},{9,13},{2,6},{6,10},{10,14},{3,7},{... | collective-permute-start | bytes 147464 | tf_op jit(solution)/shard_map/ppermute | solution.py:20
  8.8 2.9 %multiply_reduce_fusion = bf16[4,4,256,256]{3,2,1,0:T(8,128)(2,1)S(1)} fusion(bf16[3,256,256]{2,1,0:T(8,128)(2,1)} %param.8, bf16[3,4,4]{2,1,0:T(4,128)(2,1)S(1)} %fusion.290), kind=kLoop, calls=%fused_computation | loop fusion | flops 5242880 | bytes 2490464 | tf_op jit(solution)/shard_map/reduce_sum | solution.py:48
  16.0 2.1 collective-permute-start.2
  20.5 2.0 collective-permute-done.3
  25.3 2.7 %collective-permute-start.4 = (bf16[24,6,6,256]{3,0,2,1:T(8,128)(2,1)S(1)}, bf16[24,6,6,256]{3,0,2,1:T(8,128)(2,1)S(1)}, u32[]{:S(2)}, u32[]{:S(2)}) collective-permute-start(bf16[24,6,6,256]{3,0,2,1:T(8,128)(2,1)S(1)} %pad_maximum_fusion), channel_id=1, source_target_pairs={{0,4},{4,0},{8,12},{12,8},{1,5},{5,1},{9,13},{13,9},{2,6},{6,2},{1... | collective-permute-start | bytes 1327112 | tf_op jit(solution)/shard_map/ppermute | solution.py:29
  29.3 7.4 %collective-permute-done.4 = bf16[24,6,6,256]{3,0,2,1:T(8,128)(2,1)S(1)} collective-permute-done((bf16[24,6,6,256]{3,0,2,1:T(8,128)(2,1)S(1)}, bf16[24,6,6,256]{3,0,2,1:T(8,128)(2,1)S(1)}, u32[]{:S(2)}, u32[]{:S(2)}) %collective-permute-start.4) | collective-permute-done | bytes 442400 | tf_op jit(solution)/shard_map/ppermute | solution.py:29
  36.6 3.1 %collective-permute-start.5 = (bf16[24,6,6,256]{3,0,2,1:T(8,128)(2,1)S(1)}, bf16[24,6,6,256]{3,0,2,1:T(8,128)(2,1)S(1)}, u32[]{:S(2)}, u32[]{:S(2)}) collective-permute-start(bf16[24,6,6,256]{3,0,2,1:T(8,128)(2,1)S(1)} %collective-permute-done.4), channel_id=1, source_target_pairs={{0,8},{4,12},{8,0},{12,4},{1,9},{5,13},{9,1},{13,5},{2,10},{6,14},... | collective-permute-start | bytes 1327112 | tf_op jit(solution)/shard_map/ppermute | solution.py:29
  41.8 17.3 %collective-permute-done.5 = bf16[24,6,6,256]{3,0,2,1:T(8,128)(2,1)S(1)} collective-permute-done((bf16[24,6,6,256]{3,0,2,1:T(8,128)(2,1)S(1)}, bf16[24,6,6,256]{3,0,2,1:T(8,128)(2,1)S(1)}, u32[]{:S(2)}, u32[]{:S(2)}) %collective-permute-start.5) | collective-permute-done | bytes 442400 | tf_op jit(solution)/shard_map/ppermute | solution.py:29
  59.8 1.9 fusion.159
  65.1 2.0 fusion.253
  72.2 2.3 fusion.331
  74.5 4.1 %collective-permute-start.6 = (bf16[24,1,4,256]{3,0,2,1:T(8,128)(2,1)S(1)}, bf16[24,1,4,256]{3,0,2,1:T(8,128)(2,1)S(1)}, u32[]{:S(2)}, u32[]{:S(2)}) collective-permute-start(bf16[24,1,4,256]{3,0,2,1:T(8,128)(2,1)S(1)} %get-tuple-element.30), channel_id=1, source_target_pairs={{0,4},{4,8},{8,12},{1,5},{5,9},{9,13},{2,6},{6,10},{10,14},{3,7},{... | collective-permute-start | bytes 147464 | tf_op jit(solution)/shard_map/ppermute | solution.py:20
  80.5 4.3 %collective-permute-done.7 = bf16[24,1,4,256]{3,0,2,1:T(8,128)(2,1)S(1)} collective-permute-done((bf16[24,1,4,256]{3,0,2,1:T(8,128)(2,1)S(1)}, bf16[24,1,4,256]{3,0,2,1:T(8,128)(2,1)S(1)}, u32[]{:S(2)}, u32[]{:S(2)}) %collective-permute-start.7) | collective-permute-done | bytes 49184 | tf_op jit(solution)/shard_map/ppermute | solution.py:21
  90.2 2.0 collective-permute-start.10
  92.6 9.3 %collective-permute-done.10 = bf16[24,6,6,256]{3,0,2,1:T(8,128)(2,1)S(1)} collective-permute-done((bf16[24,6,6,256]{3,0,2,1:T(8,128)(2,1)S(1)}, bf16[24,6,6,256]{3,0,2,1:T(8,128)(2,1)S(1)}, u32[]{:S(2)}, u32[]{:S(2)}) %collective-permute-start.10) | collective-permute-done | bytes 442400 | tf_op jit(solution)/shard_map/ppermute | solution.py:29
  101.9 3.6 %collective-permute-start.11 = (bf16[24,6,6,256]{3,0,2,1:T(8,128)(2,1)S(1)}, bf16[24,6,6,256]{3,0,2,1:T(8,128)(2,1)S(1)}, u32[]{:S(2)}, u32[]{:S(2)}) collective-permute-start(bf16[24,6,6,256]{3,0,2,1:T(8,128)(2,1)S(1)} %collective-permute-done.10), channel_id=1, source_target_pairs={{0,8},{4,12},{8,0},{12,4},{1,9},{5,13},{9,1},{13,5},{2,10},{6,14},... | collective-permute-start | bytes 1327112 | tf_op jit(solution)/shard_map/ppermute | solution.py:29
  106.7 19.0 %collective-permute-done.11 = bf16[24,6,6,256]{3,0,2,1:T(8,128)(2,1)S(1)} collective-permute-done((bf16[24,6,6,256]{3,0,2,1:T(8,128)(2,1)S(1)}, bf16[24,6,6,256]{3,0,2,1:T(8,128)(2,1)S(1)}, u32[]{:S(2)}, u32[]{:S(2)}) %collective-permute-start.11) | collective-permute-done | bytes 442400 | tf_op jit(solution)/shard_map/ppermute | solution.py:29
  128.4 1.9 fusion.146
  131.8 2.0 fusion.252
  138.9 2.6 fusion.332
  144.6 4.3 %collective-permute-done.13 = bf16[24,1,4,256]{3,0,2,1:T(8,128)(2,1)S(1)} collective-permute-done((bf16[24,1,4,256]{3,0,2,1:T(8,128)(2,1)S(1)}, bf16[24,1,4,256]{3,0,2,1:T(8,128)(2,1)S(1)}, u32[]{:S(2)}, u32[]{:S(2)}) %collective-permute-start.13) | collective-permute-done | bytes 49184 | tf_op jit(solution)/shard_map/ppermute | solution.py:21
  156.6 9.6 %collective-permute-done.16 = bf16[24,6,6,256]{3,0,2,1:T(8,128)(2,1)S(1)} collective-permute-done((bf16[24,6,6,256]{3,0,2,1:T(8,128)(2,1)S(1)}, bf16[24,6,6,256]{3,0,2,1:T(8,128)(2,1)S(1)}, u32[]{:S(2)}, u32[]{:S(2)}) %collective-permute-start.16) | collective-permute-done | bytes 442400 | tf_op jit(solution)/shard_map/ppermute | solution.py:29
  166.2 3.5 %collective-permute-start.17 = (bf16[24,6,6,256]{3,0,2,1:T(8,128)(2,1)S(1)}, bf16[24,6,6,256]{3,0,2,1:T(8,128)(2,1)S(1)}, u32[]{:S(2)}, u32[]{:S(2)}) collective-permute-start(bf16[24,6,6,256]{3,0,2,1:T(8,128)(2,1)S(1)} %collective-permute-done.16), channel_id=1, source_target_pairs={{0,8},{4,12},{8,0},{12,4},{1,9},{5,13},{9,1},{13,5},{2,10},{6,14},... | collective-permute-start | bytes 1327112 | tf_op jit(solution)/shard_map/ppermute | solution.py:29
  170.9 19.3 %collective-permute-done.17 = bf16[24,6,6,256]{3,0,2,1:T(8,128)(2,1)S(1)} collective-permute-done((bf16[24,6,6,256]{3,0,2,1:T(8,128)(2,1)S(1)}, bf16[24,6,6,256]{3,0,2,1:T(8,128)(2,1)S(1)}, u32[]{:S(2)}, u32[]{:S(2)}) %collective-permute-start.17) | collective-permute-done | bytes 442400 | tf_op jit(solution)/shard_map/ppermute | solution.py:29
  191.0 1.9 fusion.129
  192.9 1.9 fusion.131
  196.3 2.0 fusion.251
  199.9 1.9 fusion.255
  208.3 4.3 %collective-permute-done.19 = bf16[24,1,4,256]{3,0,2,1:T(8,128)(2,1)S(1)} collective-permute-done((bf16[24,1,4,256]{3,0,2,1:T(8,128)(2,1)S(1)}, bf16[24,1,4,256]{3,0,2,1:T(8,128)(2,1)S(1)}, u32[]{:S(2)}, u32[]{:S(2)}) %collective-permute-start.19) | collective-permute-done | bytes 49184 | tf_op jit(solution)/shard_map/ppermute | solution.py:21
  220.3 9.6 %collective-permute-done.22 = bf16[24,6,6,256]{3,0,2,1:T(8,128)(2,1)S(1)} collective-permute-done((bf16[24,6,6,256]{3,0,2,1:T(8,128)(2,1)S(1)}, bf16[24,6,6,256]{3,0,2,1:T(8,128)(2,1)S(1)}, u32[]{:S(2)}, u32[]{:S(2)}) %collective-permute-start.22) | collective-permute-done | bytes 442400 | tf_op jit(solution)/shard_map/ppermute | solution.py:29
  229.9 3.5 %collective-permute-start.23 = (bf16[24,6,6,256]{3,0,2,1:T(8,128)(2,1)S(1)}, bf16[24,6,6,256]{3,0,2,1:T(8,128)(2,1)S(1)}, u32[]{:S(2)}, u32[]{:S(2)}) collective-permute-start(bf16[24,6,6,256]{3,0,2,1:T(8,128)(2,1)S(1)} %collective-permute-done.22), channel_id=1, source_target_pairs={{0,8},{4,12},{8,0},{12,4},{1,9},{5,13},{9,1},{13,5},{2,10},{6,14},... | collective-permute-start | bytes 1327112 | tf_op jit(solution)/shard_map/ppermute | solution.py:29
  233.9 20.0 %collective-permute-done.23 = bf16[24,6,6,256]{3,0,2,1:T(8,128)(2,1)S(1)} collective-permute-done((bf16[24,6,6,256]{3,0,2,1:T(8,128)(2,1)S(1)}, bf16[24,6,6,256]{3,0,2,1:T(8,128)(2,1)S(1)}, u32[]{:S(2)}, u32[]{:S(2)}) %collective-permute-start.23) | collective-permute-done | bytes 442400 | tf_op jit(solution)/shard_map/ppermute | solution.py:29
  (141 shorter events, 77.5 us)
Async XLA Ops:
  1.9 13.4 %collective-permute-start = (bf16[24,1,4,256]{3,0,2,1:T(8,128)(2,1)S(1)}, bf16[24,1,4,256]{3,0,2,1:T(8,128)(2,1)S(1)}, u32[]{:S(2)}, u32[]{:S(2)}) collective-permute-start(bf16[24,1,4,256]{3,0,2,1:T(8,128)(2,1)S(1)} %get-tuple-element.32), channel_id=1, source_target_pairs={{0,4},{4,8},{8,12},{1,5},{5,9},{9,13},{2,6},{6,10},{10,14},{3,7},{... | collective-permute-start | bytes 147464 | tf_op jit(solution)/shard_map/ppermute | solution.py:20
  6.8 8.5 %collective-permute-start.1 = (bf16[24,1,4,256]{3,0,2,1:T(8,128)(2,1)S(1)}, bf16[24,1,4,256]{3,0,2,1:T(8,128)(2,1)S(1)}, u32[]{:S(2)}, u32[]{:S(2)}) collective-permute-start(bf16[24,1,4,256]{3,0,2,1:T(8,128)(2,1)S(1)} %get-tuple-element.33), channel_id=1, source_target_pairs={{4,0},{8,4},{12,8},{5,1},{9,5},{13,9},{6,2},{10,6},{14,10},{7,3},{... | collective-permute-start | bytes 147464 | tf_op jit(solution)/shard_map/ppermute | solution.py:21
  16.0 4.5 %collective-permute-start.2 = (bf16[24,6,1,256]{3,0,2,1:T(8,128)(2,1)}, bf16[24,6,1,256]{3,0,2,1:T(8,128)(2,1)}, u32[]{:S(2)}, u32[]{:S(2)}) collective-permute-start(bf16[24,6,1,256]{3,0,2,1:T(8,128)(2,1)} %get-tuple-element.24), channel_id=1, source_target_pairs={{0,1},{1,2},{2,3},{4,5},{5,6},{6,7},{8,9},{9,10},{10,11},{12,13},{... | collective-permute-start | bytes 221192 | tf_op jit(solution)/shard_map/ppermute | solution.py:20
  18.1 4.4 %collective-permute-start.3 = (bf16[24,6,1,256]{3,0,2,1:T(8,128)(2,1)}, bf16[24,6,1,256]{3,0,2,1:T(8,128)(2,1)}, u32[]{:S(2)}, u32[]{:S(2)}) collective-permute-start(bf16[24,6,1,256]{3,0,2,1:T(8,128)(2,1)} %get-tuple-element.25), channel_id=1, source_target_pairs={{1,0},{2,1},{3,2},{5,4},{6,5},{7,6},{9,8},{10,9},{11,10},{13,12},{... | collective-permute-start | bytes 221192 | tf_op jit(solution)/shard_map/ppermute | solution.py:21
  25.3 11.4 %collective-permute-start.4 = (bf16[24,6,6,256]{3,0,2,1:T(8,128)(2,1)S(1)}, bf16[24,6,6,256]{3,0,2,1:T(8,128)(2,1)S(1)}, u32[]{:S(2)}, u32[]{:S(2)}) collective-permute-start(bf16[24,6,6,256]{3,0,2,1:T(8,128)(2,1)S(1)} %pad_maximum_fusion), channel_id=1, source_target_pairs={{0,4},{4,0},{8,12},{12,8},{1,5},{5,1},{9,13},{13,9},{2,6},{6,2},{1... | collective-permute-start | bytes 1327112 | tf_op jit(solution)/shard_map/ppermute | solution.py:29
  36.6 22.4 %collective-permute-start.5 = (bf16[24,6,6,256]{3,0,2,1:T(8,128)(2,1)S(1)}, bf16[24,6,6,256]{3,0,2,1:T(8,128)(2,1)S(1)}, u32[]{:S(2)}, u32[]{:S(2)}) collective-permute-start(bf16[24,6,6,256]{3,0,2,1:T(8,128)(2,1)S(1)} %collective-permute-done.4), channel_id=1, source_target_pairs={{0,8},{4,12},{8,0},{12,4},{1,9},{5,13},{9,1},{13,5},{2,10},{6,14},... | collective-permute-start | bytes 1327112 | tf_op jit(solution)/shard_map/ppermute | solution.py:29
  65.1 7.1 %copy-start.10 = (f32[24,4,4,256]{3,0,2,1:T(8,128)S(1)}, f32[24,4,4,256]{3,0,2,1:T(8,128)}, u32[]{:S(2)}) copy-start(f32[24,4,4,256]{3,0,2,1:T(8,128)} %fusion.159) | copy-start | bytes 1179652
  65.1 7.1 %copy-start.11 = (f32[24,4,4,256]{3,0,2,1:T(8,128)S(1)}, f32[24,4,4,256]{3,0,2,1:T(8,128)}, u32[]{:S(2)}) copy-start(f32[24,4,4,256]{3,0,2,1:T(8,128)} %fusion.161) | copy-start | bytes 1179652
  74.5 5.9 %collective-permute-start.6 = (bf16[24,1,4,256]{3,0,2,1:T(8,128)(2,1)S(1)}, bf16[24,1,4,256]{3,0,2,1:T(8,128)(2,1)S(1)}, u32[]{:S(2)}, u32[]{:S(2)}) collective-permute-start(bf16[24,1,4,256]{3,0,2,1:T(8,128)(2,1)S(1)} %get-tuple-element.30), channel_id=1, source_target_pairs={{0,4},{4,8},{8,12},{1,5},{5,9},{9,13},{2,6},{6,10},{10,14},{3,7},{... | collective-permute-start | bytes 147464 | tf_op jit(solution)/shard_map/ppermute | solution.py:20
  78.6 8.8 %copy-start.1 = (bf16[9,256,256]{2,1,0:T(8,128)(2,1)S(1)}, bf16[9,256,256]{2,1,0:T(8,128)(2,1)}, u32[]{:S(2)}) copy-start(bf16[9,256,256]{2,1,0:T(8,128)(2,1)} %param.6) | copy-start | bytes 3538948
  78.6 6.1 %collective-permute-start.7 = (bf16[24,1,4,256]{3,0,2,1:T(8,128)(2,1)S(1)}, bf16[24,1,4,256]{3,0,2,1:T(8,128)(2,1)S(1)}, u32[]{:S(2)}, u32[]{:S(2)}) collective-permute-start(bf16[24,1,4,256]{3,0,2,1:T(8,128)(2,1)S(1)} %get-tuple-element.31), channel_id=1, source_target_pairs={{4,0},{8,4},{12,8},{5,1},{9,5},{13,9},{6,2},{10,6},{14,10},{7,3},{... | collective-permute-start | bytes 147464 | tf_op jit(solution)/shard_map/ppermute | solution.py:21
  84.8 2.8 %collective-permute-start.8 = (bf16[24,6,1,256]{3,0,2,1:T(8,128)(2,1)S(1)}, bf16[24,6,1,256]{3,0,2,1:T(8,128)(2,1)S(1)}, u32[]{:S(2)}, u32[]{:S(2)}) collective-permute-start(bf16[24,6,1,256]{3,0,2,1:T(8,128)(2,1)S(1)} %get-tuple-element.22), channel_id=1, source_target_pairs={{0,1},{1,2},{2,3},{4,5},{5,6},{6,7},{8,9},{9,10},{10,11},{12,13},{... | collective-permute-start | bytes 221192 | tf_op jit(solution)/shard_map/ppermute | solution.py:20
  86.1 3.2 %collective-permute-start.9 = (bf16[24,6,1,256]{3,0,2,1:T(8,128)(2,1)S(1)}, bf16[24,6,1,256]{3,0,2,1:T(8,128)(2,1)S(1)}, u32[]{:S(2)}, u32[]{:S(2)}) collective-permute-start(bf16[24,6,1,256]{3,0,2,1:T(8,128)(2,1)S(1)} %get-tuple-element.23), channel_id=1, source_target_pairs={{1,0},{2,1},{3,2},{5,4},{6,5},{7,6},{9,8},{10,9},{11,10},{13,12},{... | collective-permute-start | bytes 221192 | tf_op jit(solution)/shard_map/ppermute | solution.py:21
  90.2 11.7 %collective-permute-start.10 = (bf16[24,6,6,256]{3,0,2,1:T(8,128)(2,1)S(1)}, bf16[24,6,6,256]{3,0,2,1:T(8,128)(2,1)S(1)}, u32[]{:S(2)}, u32[]{:S(2)}) collective-permute-start(bf16[24,6,6,256]{3,0,2,1:T(8,128)(2,1)S(1)} %pad_maximum_fusion.1), channel_id=1, source_target_pairs={{0,4},{4,0},{8,12},{12,8},{1,5},{5,1},{9,13},{13,9},{2,6},{6,2},{1... | collective-permute-start | bytes 1327112 | tf_op jit(solution)/shard_map/ppermute | solution.py:29
  101.9 23.8 %collective-permute-start.11 = (bf16[24,6,6,256]{3,0,2,1:T(8,128)(2,1)S(1)}, bf16[24,6,6,256]{3,0,2,1:T(8,128)(2,1)S(1)}, u32[]{:S(2)}, u32[]{:S(2)}) collective-permute-start(bf16[24,6,6,256]{3,0,2,1:T(8,128)(2,1)S(1)} %collective-permute-done.10), channel_id=1, source_target_pairs={{0,8},{4,12},{8,0},{12,4},{1,9},{5,13},{9,1},{13,5},{2,10},{6,14},... | collective-permute-start | bytes 1327112 | tf_op jit(solution)/shard_map/ppermute | solution.py:29
  131.8 7.1 %copy-start.9 = (f32[24,4,4,256]{3,0,2,1:T(8,128)S(1)}, f32[24,4,4,256]{3,0,2,1:T(8,128)}, u32[]{:S(2)}) copy-start(f32[24,4,4,256]{3,0,2,1:T(8,128)} %fusion.144) | copy-start | bytes 1179652
  141.4 3.1 %collective-permute-start.12 = (bf16[24,1,4,256]{3,0,2,1:T(8,128)(2,1)S(1)}, bf16[24,1,4,256]{3,0,2,1:T(8,128)(2,1)S(1)}, u32[]{:S(2)}, u32[]{:S(2)}) collective-permute-start(bf16[24,1,4,256]{3,0,2,1:T(8,128)(2,1)S(1)} %get-tuple-element.28), channel_id=1, source_target_pairs={{0,4},{4,8},{8,12},{1,5},{5,9},{9,13},{2,6},{6,10},{10,14},{3,7},{... | collective-permute-start | bytes 147464 | tf_op jit(solution)/shard_map/ppermute | solution.py:20
  142.7 8.8 %copy-start.2 = (bf16[9,256,256]{2,1,0:T(8,128)(2,1)S(1)}, bf16[9,256,256]{2,1,0:T(8,128)(2,1)}, u32[]{:S(2)}) copy-start(bf16[9,256,256]{2,1,0:T(8,128)(2,1)} %param.6) | copy-start | bytes 3538948
  142.8 6.1 %collective-permute-start.13 = (bf16[24,1,4,256]{3,0,2,1:T(8,128)(2,1)S(1)}, bf16[24,1,4,256]{3,0,2,1:T(8,128)(2,1)S(1)}, u32[]{:S(2)}, u32[]{:S(2)}) collective-permute-start(bf16[24,1,4,256]{3,0,2,1:T(8,128)(2,1)S(1)} %get-tuple-element.29), channel_id=1, source_target_pairs={{4,0},{8,4},{12,8},{5,1},{9,5},{13,9},{6,2},{10,6},{14,10},{7,3},{... | collective-permute-start | bytes 147464 | tf_op jit(solution)/shard_map/ppermute | solution.py:21
  148.9 2.8 %collective-permute-start.14 = (bf16[24,6,1,256]{3,0,2,1:T(8,128)(2,1)S(1)}, bf16[24,6,1,256]{3,0,2,1:T(8,128)(2,1)S(1)}, u32[]{:S(2)}, u32[]{:S(2)}) collective-permute-start(bf16[24,6,1,256]{3,0,2,1:T(8,128)(2,1)S(1)} %get-tuple-element.20), channel_id=1, source_target_pairs={{0,1},{1,2},{2,3},{4,5},{5,6},{6,7},{8,9},{9,10},{10,11},{12,13},{... | collective-permute-start | bytes 221192 | tf_op jit(solution)/shard_map/ppermute | solution.py:20
  150.2 3.2 %collective-permute-start.15 = (bf16[24,6,1,256]{3,0,2,1:T(8,128)(2,1)S(1)}, bf16[24,6,1,256]{3,0,2,1:T(8,128)(2,1)S(1)}, u32[]{:S(2)}, u32[]{:S(2)}) collective-permute-start(bf16[24,6,1,256]{3,0,2,1:T(8,128)(2,1)S(1)} %get-tuple-element.21), channel_id=1, source_target_pairs={{1,0},{2,1},{3,2},{5,4},{6,5},{7,6},{9,8},{10,9},{11,10},{13,12},{... | collective-permute-start | bytes 221192 | tf_op jit(solution)/shard_map/ppermute | solution.py:21
  154.3 11.9 %collective-permute-start.16 = (bf16[24,6,6,256]{3,0,2,1:T(8,128)(2,1)S(1)}, bf16[24,6,6,256]{3,0,2,1:T(8,128)(2,1)S(1)}, u32[]{:S(2)}, u32[]{:S(2)}) collective-permute-start(bf16[24,6,6,256]{3,0,2,1:T(8,128)(2,1)S(1)} %pad_maximum_fusion.2), channel_id=1, source_target_pairs={{0,4},{4,0},{8,12},{12,8},{1,5},{5,1},{9,13},{13,9},{2,6},{6,2},{1... | collective-permute-start | bytes 1327112 | tf_op jit(solution)/shard_map/ppermute | solution.py:29
  166.2 23.9 %collective-permute-start.17 = (bf16[24,6,6,256]{3,0,2,1:T(8,128)(2,1)S(1)}, bf16[24,6,6,256]{3,0,2,1:T(8,128)(2,1)S(1)}, u32[]{:S(2)}, u32[]{:S(2)}) collective-permute-start(bf16[24,6,6,256]{3,0,2,1:T(8,128)(2,1)S(1)} %collective-permute-done.16), channel_id=1, source_target_pairs={{0,8},{4,12},{8,0},{12,4},{1,9},{5,13},{9,1},{13,5},{2,10},{6,14},... | collective-permute-start | bytes 1327112 | tf_op jit(solution)/shard_map/ppermute | solution.py:29
  196.3 7.2 %copy-start.7 = (f32[24,4,4,256]{3,0,2,1:T(8,128)S(1)}, f32[24,4,4,256]{3,0,2,1:T(8,128)}, u32[]{:S(2)}) copy-start(f32[24,4,4,256]{3,0,2,1:T(8,128)} %fusion.129) | copy-start | bytes 1179652
  196.3 7.2 %copy-start.8 = (f32[24,4,4,256]{3,0,2,1:T(8,128)S(1)}, f32[24,4,4,256]{3,0,2,1:T(8,128)}, u32[]{:S(2)}) copy-start(f32[24,4,4,256]{3,0,2,1:T(8,128)} %fusion.131) | copy-start | bytes 1179652
  205.2 3.1 %collective-permute-start.18 = (bf16[24,1,4,256]{3,0,2,1:T(8,128)(2,1)S(1)}, bf16[24,1,4,256]{3,0,2,1:T(8,128)(2,1)S(1)}, u32[]{:S(2)}, u32[]{:S(2)}) collective-permute-start(bf16[24,1,4,256]{3,0,2,1:T(8,128)(2,1)S(1)} %get-tuple-element.26), channel_id=1, source_target_pairs={{0,4},{4,8},{8,12},{1,5},{5,9},{9,13},{2,6},{6,10},{10,14},{3,7},{... | collective-permute-start | bytes 147464 | tf_op jit(solution)/shard_map/ppermute | solution.py:20
  206.5 8.8 %copy-start.3 = (bf16[9,256,256]{2,1,0:T(8,128)(2,1)S(1)}, bf16[9,256,256]{2,1,0:T(8,128)(2,1)}, u32[]{:S(2)}) copy-start(bf16[9,256,256]{2,1,0:T(8,128)(2,1)} %param.6) | copy-start | bytes 3538948
  206.5 6.1 %collective-permute-start.19 = (bf16[24,1,4,256]{3,0,2,1:T(8,128)(2,1)S(1)}, bf16[24,1,4,256]{3,0,2,1:T(8,128)(2,1)S(1)}, u32[]{:S(2)}, u32[]{:S(2)}) collective-permute-start(bf16[24,1,4,256]{3,0,2,1:T(8,128)(2,1)S(1)} %get-tuple-element.27), channel_id=1, source_target_pairs={{4,0},{8,4},{12,8},{5,1},{9,5},{13,9},{6,2},{10,6},{14,10},{7,3},{... | collective-permute-start | bytes 147464 | tf_op jit(solution)/shard_map/ppermute | solution.py:21
  212.6 3.7 %collective-permute-start.20 = (bf16[24,6,1,256]{3,0,2,1:T(8,128)(2,1)S(1)}, bf16[24,6,1,256]{3,0,2,1:T(8,128)(2,1)S(1)}, u32[]{:S(2)}, u32[]{:S(2)}) collective-permute-start(bf16[24,6,1,256]{3,0,2,1:T(8,128)(2,1)S(1)} %get-tuple-element.18), channel_id=1, source_target_pairs={{0,1},{1,2},{2,3},{4,5},{5,6},{6,7},{8,9},{9,10},{10,11},{12,13},{... | collective-permute-start | bytes 221192 | tf_op jit(solution)/shard_map/ppermute | solution.py:20
  213.9 3.2 %collective-permute-start.21 = (bf16[24,6,1,256]{3,0,2,1:T(8,128)(2,1)S(1)}, bf16[24,6,1,256]{3,0,2,1:T(8,128)(2,1)S(1)}, u32[]{:S(2)}, u32[]{:S(2)}) collective-permute-start(bf16[24,6,1,256]{3,0,2,1:T(8,128)(2,1)S(1)} %get-tuple-element.19), channel_id=1, source_target_pairs={{1,0},{2,1},{3,2},{5,4},{6,5},{7,6},{9,8},{10,9},{11,10},{13,12},{... | collective-permute-start | bytes 221192 | tf_op jit(solution)/shard_map/ppermute | solution.py:21
  218.0 12.0 %collective-permute-start.22 = (bf16[24,6,6,256]{3,0,2,1:T(8,128)(2,1)S(1)}, bf16[24,6,6,256]{3,0,2,1:T(8,128)(2,1)S(1)}, u32[]{:S(2)}, u32[]{:S(2)}) collective-permute-start(bf16[24,6,6,256]{3,0,2,1:T(8,128)(2,1)S(1)} %pad_maximum_fusion.3), channel_id=1, source_target_pairs={{0,4},{4,0},{8,12},{12,8},{1,5},{5,1},{9,13},{13,9},{2,6},{6,2},{1... | collective-permute-start | bytes 1327112 | tf_op jit(solution)/shard_map/ppermute | solution.py:29
  229.9 24.0 %collective-permute-start.23 = (bf16[24,6,6,256]{3,0,2,1:T(8,128)(2,1)S(1)}, bf16[24,6,6,256]{3,0,2,1:T(8,128)(2,1)S(1)}, u32[]{:S(2)}, u32[]{:S(2)}) collective-permute-start(bf16[24,6,6,256]{3,0,2,1:T(8,128)(2,1)S(1)} %collective-permute-done.22), channel_id=1, source_target_pairs={{0,8},{4,12},{8,0},{12,4},{1,9},{5,13},{9,1},{13,5},{2,10},{6,14},... | collective-permute-start | bytes 1327112 | tf_op jit(solution)/shard_map/ppermute | solution.py:29
  (5 other events, 18.4 us)
where the time goes:
time: 259 us; the launch traced here: 258 us
  waiting for transfers between devices  130 us (50%)
  starting transfers between devices  50.2 us (19%)
  matrix products  47.4 us (18%)
  local copies, waits for them, and re-layouts  21.7 us (8%)
  other arithmetic  6.88 us (3%)
    ppermute x8, waiting for transfers between devices, swapped(): return lax.ppermute(value, axis, pairs)  111 us
    dot_general x56, matrix products, block_product(): jnp.einsum('vxyb,bc->vxyc', slab, matrix, preferred_element_type=jnp.floa...  45.1 us
    ppermute x8, starting transfers between devices, swapped(): return lax.ppermute(value, axis, pairs)  22 us
    ppermute x8, waiting for transfers between devices, with_halo(): after = lax.ppermute(leading, axis, down)  18.8 us
    ppermute x8, starting transfers between devices, with_halo(): before = lax.ppermute(last, axis, up)  17.5 us
    dynamic_slice x16, local copies, waits for them, and re-layouts, window(): lax.dynamic_slice(padded, starts, (vectors, count_x, count_y, orbitals))  15 us
    ppermute x8, starting transfers between devices, with_halo(): after = lax.ppermute(leading, axis, down)  10.7 us
  transfers between devices with their start and end apart: 24, of which 15 were waited for; matrix products, arithmetic and copies ran while one was open for 7% of the time, Pallas kernels for 0%

commit v1 on v0

--- a/solution.py
+++ b/solution.py
@@ -1,7 +1,13 @@
+import functools
+
 import jax
 import jax.numpy as jnp
 from jax import lax
+from jax.experimental import pallas as pl
+from jax.experimental.pallas import tpu as pltpu
 from jax.sharding import PartitionSpec as P
+
+MESH = pl.DeviceIdType.MESH
 
 ITERS = 4
 
@@ -79,7 +85,311 @@
     return (current, previous)
 
 
+CHIP_VECTORS = 3
+SLOTS = 2
+
+
+def home_row(out_row, half, rows, wide_len, row_len):
+    x = out_row // (2 * rows)
+    sector = (out_row // rows) % 2
+    y = out_row % rows
+    column = jnp.where(sector == 0, x, 2 * half - 1 - x)
+    domains = rows // row_len
+    return ((column // wide_len) * domains + y // row_len) * (wide_len * row_len) + (column % wide_len) * row_len + y % row_len
+
+
+def vector_kernel(
+    sizes, r0, reg, hop, pair, onsite, out,
+    recv, regs, wn, wp, wpt, buf, previous, current, stage, kind,
+    send_sem, recv_sem, rsend_sem, rrecv_sem, osend_sem, orecv_sem, weight_sem,
+):
+    wide, trans, sub, wide_len, row_len = sizes
+    domains = trans * sub
+    sources = wide * domains
+    half = wide * wide_len // 2
+    rows = domains * row_len
+    cells = 2 * half * rows
+    count, orbitals = r0.shape[0], r0.shape[2]
+    total = SLOTS * cells
+    group = lax.axis_index("groups")
+    z, t, c = lax.axis_index("wide"), lax.axis_index("trans"), lax.axis_index("sub")
+    me = z * domains + t * sub + c
+    my_first = (z * trans + t) * CHIP_VECTORS + c * SLOTS
+    my_slots = SLOTS - c
+
+    def device(index):
+        return (group, index // domains, (index % domains) // sub, index % sub)
+
+    def owner(v):
+        chip, place = v // CHIP_VECTORS, v % CHIP_VECTORS
+        return chip * sub + place // SLOTS, place % SLOTS
+
+    loads = [
+        pltpu.make_async_copy(hop, wn.at[pl.ds(0, 9)], weight_sem.at[0]),
+        pltpu.make_async_copy(onsite, wn.at[pl.ds(9, 3)], weight_sem.at[1]),
+        pltpu.make_async_copy(pair, wp, weight_sem.at[2]),
+    ]
+    for load in loads:
+        load.start()
+
+    barrier = pltpu.get_barrier_semaphore()
+
+    def greet(j, carry):
+        pl.semaphore_signal(barrier, inc=1, device_id=device((me + j) % sources), device_id_type=MESH)
+        return carry
+
+    lax.fori_loop(1, sources, greet, 0)
+    pl.semaphore_wait(barrier, sources - 1)
+
+    def region_copy(to, frm):
+        return pltpu.make_async_remote_copy(
+            src_ref=reg, dst_ref=regs.at[frm], send_sem=rsend_sem.at[to], recv_sem=rrecv_sem.at[frm],
+            device_id=device(to), device_id_type=MESH,
+        )
+
+    def vector_copy(v, frm):
+        to, slot = owner(v)
+        return pltpu.make_async_remote_copy(
+            src_ref=r0.at[v], dst_ref=recv.at[slot, frm], send_sem=send_sem.at[v], recv_sem=recv_sem.at[slot, frm],
+            device_id=device(to), device_id_type=MESH,
+        )
+
+    def send_vector(j, carry):
+        v = (my_first + j + count // 2) % count
+
+        @pl.when(owner(v)[0] != me)
+        def _():
+            vector_copy(v, me).start()
+
+        return carry
+
+    lax.fori_loop(0, count, send_vector, 0)
+
+    def send_region(j, carry):
+        region_copy((me + j) % sources, me).start()
+        return carry
+
+    lax.fori_loop(1, sources, send_region, 0)
+
+    regs[me] = reg[...]
+    recv[0, me] = r0[my_first]
+
+    @pl.when(c == 0)
+    def _():
+        recv[1, me] = r0[my_first + 1]
+
+    @pl.when(c != 0)
+    def _():
+        recv[1] = jnp.zeros(recv.shape[1:], recv.dtype)
+
+    buf[:, 0] = jnp.zeros((3,) + buf.shape[2:], buf.dtype)
+    previous[...] = jnp.zeros(previous.shape, jnp.float32)
+    for load in loads:
+        load.wait()
+    for k in range(5):
+        wpt[k] = wp[k].T
+
+    lattice = lax.broadcasted_iota(jnp.int32, (cells, cells), 0)
+    home = lax.broadcasted_iota(jnp.int32, (cells, cells), 1)
+    to_lattice = (home_row(lattice, half, rows, wide_len, row_len) == home).astype(jnp.bfloat16)
+
+    def wait_region(j, carry):
+        frm = (me + j) % sources
+        region_copy(frm, frm).wait_recv()
+        return carry
+
+    def wait_vector(j, carry):
+        frm = (me + j) % sources
+        for slot in range(SLOTS):
+
+            @pl.when(slot < my_slots)
+            def _():
+                vector_copy(my_first + slot, frm).wait_recv()
+
+        return carry
+
+    lax.fori_loop(1, sources, wait_region, 0)
+    per = wide_len * row_len
+    spots = lax.broadcasted_iota(jnp.int32, (cells, sources), 0)
+    spots = home_row(spots, half, rows, wide_len, row_len)
+    picks = (spots // per == lax.broadcasted_iota(jnp.int32, (cells, sources), 1)).astype(jnp.float32)
+    spread = jnp.dot(picks, regs[...].reshape(sources, reg.shape[1]), preferred_element_type=jnp.float32)
+    lanes = lax.broadcasted_iota(jnp.int32, spread.shape, 1)
+    places = lax.broadcasted_iota(jnp.int32, spread.shape, 0)
+    places = home_row(places, half, rows, wide_len, row_len) % per
+    kinds = jnp.sum(jnp.where(lanes == places, spread, 0.0), axis=1, keepdims=True)
+    kinds = jnp.broadcast_to(kinds, (cells, orbitals)).reshape(2 * half, 1, rows, orbitals)
+    kinds = jnp.concatenate([kinds] * SLOTS, axis=1)
+    kind[...] = kinds.reshape(total, orbitals).astype(jnp.bfloat16)
+    lax.fori_loop(1, sources, wait_vector, 0)
+
+    parts = []
+    for slot in range(SLOTS):
+        part = jnp.dot(to_lattice, recv[slot].reshape(cells, orbitals), preferred_element_type=jnp.float32)
+        parts.append(part.reshape(half * 2, 1, rows, orbitals))
+    current[...] = jnp.concatenate(parts, axis=1).reshape(total, orbitals)
+
+    def store_fields():
+        field = current[...]
+        y = lax.broadcasted_iota(jnp.int32, field.shape, 0) % rows
+        below = jnp.where(y == 0, 0.0, pltpu.roll(field, 1, 0))
+        above = jnp.where(y == rows - 1, 0.0, pltpu.roll(field, total - 1, 0))
+        for index, value in enumerate((below, field, above)):
+            value = value.astype(jnp.bfloat16).reshape((half, 2, SLOTS * rows, orbitals))
+            buf[index, 1 : half + 1] = value
+            buf[index, half + 1, 0] = value[half - 1, 1]
+            buf[index, half + 1, 1] = value[half - 1, 0]
+
+    def out_copy(which, slot, to, v):
+        return pltpu.make_async_remote_copy(
+            src_ref=stage.at[which, slot, to], dst_ref=out.at[which, v],
+            send_sem=osend_sem.at[which, slot, to], recv_sem=orecv_sem.at[which, v],
+            device_id=device(to), device_id_type=MESH,
+        )
+
+    def send_home(which, values):
+        values = values.reshape(2 * half, SLOTS, rows, orbitals)
+        for slot in range(SLOTS):
+            part = lax.dot_general(
+                to_lattice, values[:, slot].reshape(cells, orbitals), (((0,), (0,)), ((), ())),
+                preferred_element_type=jnp.float32,
+            )
+            stage[which, slot] = part.astype(jnp.bfloat16).reshape(stage.shape[2:])
+
+            @pl.when(slot < my_slots)
+            def _():
+                out[which, my_first + slot] = stage[which, slot, me]
+
+        def send(j, carry):
+            to = (me + j) % sources
+            for slot in range(SLOTS):
+
+                @pl.when(slot < my_slots)
+                def _():
+                    out_copy(which, slot, to, my_first + slot).start()
+
+            return carry
+
+        lax.fori_loop(1, sources, send, 0)
+
+    def slab(a, b):
+        return buf[b + 1, 1 + a : 1 + a + half].reshape(total, orbitals)
+
+    def sector_slab(a, b, sector):
+        return buf[b + 1, 1 + a : 1 + a + half, sector].reshape(total // 2, orbitals)
+
+    def apply(carry_scale, carry_old):
+        normal = jnp.dot(slab(*HOP_OFFSETS[0]), wn[0], preferred_element_type=jnp.float32)
+        for k in range(1, 9):
+            normal = normal + jnp.dot(slab(*HOP_OFFSETS[k]), wn[k], preferred_element_type=jnp.float32)
+        for r in range(3):
+            chosen = jnp.where(kind[...] == r, slab(0, 0), jnp.zeros((), jnp.bfloat16))
+            normal = normal + jnp.dot(chosen, wn[9 + r], preferred_element_type=jnp.float32)
+        to_e = jnp.zeros((total // 2, orbitals), jnp.float32)
+        to_h = jnp.zeros((total // 2, orbitals), jnp.float32)
+        for k, (a, b) in enumerate(PAIR_OFFSETS):
+            to_e = to_e + jnp.dot(sector_slab(a, b, 1), wp[k], preferred_element_type=jnp.float32)
+            to_h = to_h + jnp.dot(sector_slab(-a, -b, 0), wpt[k], preferred_element_type=jnp.float32)
+        shape = (half, SLOTS * rows, orbitals)
+        normal = normal.reshape(half, 2, SLOTS * rows, orbitals)
+        new_e = normal[:, 0] + to_e.reshape(shape)
+        new_h = to_h.reshape(shape) - normal[:, 1]
+        new = jnp.stack([new_e, new_h], axis=1).reshape(total, orbitals)
+        new = carry_scale * new - carry_old * previous[...]
+        previous[...] = current[...]
+        current[...] = new
+
+    def step(it, carry):
+        store_fields()
+
+        @pl.when(it == ITERS - 1)
+        def _():
+            send_home(1, slab(0, 0))
+
+        first = it == 0
+        apply(jnp.where(first, 1.0, 2.0), jnp.where(first, 0.0, 1.0))
+        return carry
+
+    lax.fori_loop(0, ITERS, step, 0)
+    send_home(0, current[...].astype(jnp.bfloat16))
+
+    def finish_out(v, carry):
+        @pl.when(owner(v)[0] != me)
+        def _():
+            vector_copy(v, me).wait_send()
+            for which in range(2):
+                out_copy(which, 0, owner(v)[0], v).wait_recv()
+
+        return carry
+
+    lax.fori_loop(0, count, finish_out, 0)
+
+    def finish_sends(j, carry):
+        to = (me + j) % sources
+        region_copy(to, me).wait_send()
+        for slot in range(SLOTS):
+
+            @pl.when(slot < my_slots)
+            def _():
+                for which in range(2):
+                    out_copy(which, slot, to, my_first + slot).wait_send()
+
+        return carry
+
+    lax.fori_loop(1, sources, finish_sends, 0)
+
+
+def by_vectors(sizes, start_vectors, hopping, pairing, onsite, region):
+    wide, trans, sub = sizes
+    count, wide_len, row_len, orbitals = start_vectors.shape
+    domains = trans * sub
+    sources, per = wide * domains, wide_len * row_len
+    half, rows = wide * wide_len // 2, domains * row_len
+    cells = 2 * half * rows
+    total = SLOTS * cells
+    rounded = start_vectors.reshape(count, per, orbitals).astype(jnp.bfloat16)
+    regions = jnp.pad(region.reshape(1, per).astype(jnp.float32), ((0, 0), (0, 128 - per)))
+    vmem = pl.BlockSpec(memory_space=pltpu.VMEM)
+    hbm = pl.BlockSpec(memory_space=pl.ANY)
+    bf16, f32 = jnp.bfloat16, jnp.float32
+    dma = pltpu.SemaphoreType.DMA
+    out = pl.pallas_call(
+        functools.partial(vector_kernel, sizes + (wide_len, row_len)),
+        out_shape=jax.ShapeDtypeStruct((2, count, per, orbitals), bf16),
+        in_specs=[vmem, vmem, hbm, hbm, hbm],
+        out_specs=vmem,
+        scratch_shapes=[
+            pltpu.VMEM((SLOTS, sources, per, orbitals), bf16),
+            pltpu.VMEM((sources, 1, 128), f32),
+            pltpu.VMEM((12, orbitals, orbitals), bf16),
+            pltpu.VMEM((5, orbitals, orbitals), bf16),
+            pltpu.VMEM((5, orbitals, orbitals), bf16),
+            pltpu.VMEM((3, half + 2, 2, SLOTS * rows, orbitals), bf16),
+            pltpu.VMEM((total, orbitals), f32),
+            pltpu.VMEM((total, orbitals), f32),
+            pltpu.VMEM((2, SLOTS, sources, per, orbitals), bf16),
+            pltpu.VMEM((total, orbitals), bf16),
+            dma((count,)),
+            dma((SLOTS, sources)),
+            dma((sources,)),
+            dma((sources,)),
+            dma((2, SLOTS, sources)),
+            dma((2, count)),
+            dma((3,)),
+        ],
+        compiler_params=pltpu.CompilerParams(
+            collective_id=0, has_side_effects=True, vmem_limit_bytes=40 * 2**20
+        ),
+    )(rounded, regions, hopping, pairing, onsite)
+    wanted = out.astype(f32).reshape((2,) + start_vectors.shape)
+    return wanted[0], wanted[1]
+
+
 def solution(mesh):
+    sizes = (mesh.shape["wide"], mesh.shape["trans"], mesh.shape["sub"])
+    per_device = shards
+    if sizes == (4, 2, 2):
+        per_device = functools.partial(by_vectors, sizes)
     in_specs = (
         P(None, ("groups", "wide"), ("trans", "sub"), None),
         P(),
@@ -91,4 +401,4 @@
         P(None, ("groups", "wide"), ("trans", "sub"), None),
         P(None, ("groups", "wide"), ("trans", "sub"), None),
     )
-    return jax.shard_map(shards, mesh=mesh, in_specs=in_specs, out_specs=out_specs, check_vma=False)
+    return jax.shard_map(per_device, mesh=mesh, in_specs=in_specs, out_specs=out_specs, check_vma=False)

time: 259 us -> 38.5 us (0.15)
  waiting for transfers between devices: 130 us -> 0 us
  starting transfers between devices: 50.2 us -> 0 us
  matrix products: 47.4 us -> 0 us
  Pallas kernels: 0 us -> 31.6 us
  local copies, waits for them, and re-layouts: 21.7 us -> 4.22 us
  other arithmetic: 6.88 us -> 1.82 us
    ppermute x24 -> x0, waiting for transfers between devices: 130 us -> none  [the longest x8 111 us: swapped(): return lax.ppermute(value, axis, pairs)]
    ppermute x24 -> x0, starting transfers between devices: 50.2 us -> none  [the longest x8 22 us: swapped(): return lax.ppermute(value, axis, pairs)]
    dot_general x60 -> x0, matrix products: 47.4 us -> none  [the longest x56 45.1 us: block_product(): jnp.einsum('vxyb,bc->vxyc', slab, matrix, preferred_element_type=jnp.floa...]
    pallas_call x0 -> x1, Pallas kernels: none -> 31.6 us  [by_vectors(): pl.pallas_call(functools.partial(vector_kernel, sizes + (wide_len, row_le...]
    dynamic_slice x16 -> x0, local copies, waits for them, and re-layouts: 15 us -> none  [window(): lax.dynamic_slice(padded, starts, (vectors, count_x, count_y, orbitals))]
    reduce_sum x1 -> x0, other arithmetic: 2.88 us -> none  [shards(): jnp.sum(chosen[:, :, :, None, None] * onsite[:, None, None, :, :], axis=0)]
  transfers between devices with their start and end apart: 24 -> 0, of which waited for: 15 -> 0; matrix products, arithmetic and copies ran while one was open for 7% -> 0% of each run, Pallas kernels for 0% -> 0%
where the time goes in v1:
time: 38.5 us; the launch traced here: 38.3 us
  Pallas kernels  31.6 us (82%)
  local copies, waits for them, and re-layouts  4.22 us (11%)
  other arithmetic  1.82 us (5%)
  between operations  0.68 us (2%)
    pallas_call x1, Pallas kernels, by_vectors(): pl.pallas_call(functools.partial(vector_kernel, sizes + (wide_len, row_le...  31.6 us
    unnamed x6, local copies, waits for them, and re-layouts  2.27 us
    squeeze x2, local copies, waits for them, and re-layouts, by_vectors(): return (wanted[0], wanted[1])  1.72 us
    convert_element_type x1, other arithmetic, by_vectors(): rounded = start_vectors.reshape(count, per, orbitals).astype(jnp.bfloat16)  1.07 us

profile of v1, /device:TPU:0, one launch (start us, length us, event | category | flops | bytes accessed | tf_op | source)
XLA Modules:
  0.0 38.3 jit_solution(13649420460694492639)
XLA Ops:
  0.6 0.0 copy-start.1
  0.6 0.7 %convert_element_type.26 = f32[4,4]{1,0:T(4,128)S(1)} convert(s32[4,4]{1,0:T(4,128)} %param.9) | non-fusion elementwise | flops 16 | bytes 128 | tf_op jit(solution)/shard_map/convert_element_type | solution.py:351
  1.4 0.1 convert_element_type.27
  1.5 1.1 %convert_element_type.24 = bf16[24,4,4,256]{3,2,1,0:T(4,128)(2,1)S(1)} convert(f32[24,4,4,256]{3,2,1,0:T(4,128)} %param.5) | non-fusion elementwise | flops 98304 | bytes 589824 | tf_op jit(solution)/shard_map/convert_element_type | solution.py:350
  2.6 0.1 convert_element_type.25.r0
  2.6 0.0 copy-done.1
  2.6 0.0 copy-start
  2.6 1.3 %copy-done = bf16[9,256,256]{2,1,0:T(8,128)(2,1)S(1)} copy-done((bf16[9,256,256]{2,1,0:T(8,128)(2,1)S(1)}, bf16[9,256,256]{2,1,0:T(8,128)(2,1)}, u32[]{:S(2)}) %copy-start) | copy-done | bytes 1179672
  3.9 0.0 copy-start.2
  3.9 1.0 %copy-done.2 = bf16[3,256,256]{2,1,0:T(8,128)(2,1)S(1)} copy-done((bf16[3,256,256]{2,1,0:T(8,128)(2,1)S(1)}, bf16[3,256,256]{2,1,0:T(8,128)(2,1)}, u32[]{:S(2)}) %copy-start.2) | copy-done | bytes 393240
  4.9 31.6 %shard_map.68 = bf16[2,24,16,256]{3,2,1,0:T(8,128)(2,1)S(1)} custom-call(bf16[24,16,256]{2,1,0:T(8,128)(2,1)S(1)} %convert_element_type.25.r0, f32[1,128]{1,0:T(1,128)S(1)} %pad.4.reg, bf16[9,256,256]{2,1,0:T(8,128)(2,1)S(1)} %copy-done, bf16[5,256,256]{2,1,0:T(8,128)(2,1)S(1)} %copy-done.1, bf16[3,256,256]{2,1,0:T(8,128)(2,1)S(1)} %copy-done.2), custom_call_target="tpu_custom_call" | custom-call | tf_op jit(solution)/shard_map/pallas_call | solution.py:356
  36.4 0.1 fusion
  36.5 0.9 %squeeze.7 = f32[24,4,4,256]{3,2,1,0:T(4,128)} reshape(f32[1,24,16,256]{3,2,1,0:T(8,128)S(1)} %get-tuple-element.2) | data formatting | bytes 786432 | tf_op jit(solution)/shard_map/squeeze | solution.py:385
  37.4 0.9 %squeeze.6 = f32[24,4,4,256]{3,2,1,0:T(4,128)} reshape(f32[1,24,16,256]{3,2,1,0:T(8,128)S(1)} %get-tuple-element.3) | data formatting | bytes 786432 | tf_op jit(solution)/shard_map/squeeze | solution.py:385
  (1 shorter events, 0.0 us)
Async XLA Ops:
  0.6 2.0 %copy-start.1 = (bf16[5,256,256]{2,1,0:T(8,128)(2,1)S(1)}, bf16[5,256,256]{2,1,0:T(8,128)(2,1)}, u32[]{:S(2)}) copy-start(bf16[5,256,256]{2,1,0:T(8,128)(2,1)} %pair.1) | copy-start | bytes 1966084
  2.6 1.3 %copy-start = (bf16[9,256,256]{2,1,0:T(8,128)(2,1)S(1)}, bf16[9,256,256]{2,1,0:T(8,128)(2,1)}, u32[]{:S(2)}) copy-start(bf16[9,256,256]{2,1,0:T(8,128)(2,1)} %hop.1) | copy-start | bytes 3538948
  3.9 1.0 %copy-start.2 = (bf16[3,256,256]{2,1,0:T(8,128)(2,1)S(1)}, bf16[3,256,256]{2,1,0:T(8,128)(2,1)}, u32[]{:S(2)}) copy-start(bf16[3,256,256]{2,1,0:T(8,128)(2,1)} %onsite.1) | copy-start | bytes 1179652

commit v2 on v1

--- a/solution.py
+++ b/solution.py
@@ -99,8 +99,8 @@
 
 
 def vector_kernel(
-    sizes, r0, reg, hop, pair, onsite, out,
-    recv, regs, wn, wp, wpt, buf, previous, current, stage, kind,
+    sizes, start, region, hop, pair, onsite, out,
+    raw, wide_raw, r0, reg_raw, reg, recv, regs, wn, wp, wpt, buf, previous, current, stage, mask,
     send_sem, recv_sem, rsend_sem, rrecv_sem, osend_sem, orecv_sem, weight_sem,
 ):
     wide, trans, sub, wide_len, row_len = sizes
@@ -110,7 +110,6 @@
     rows = domains * row_len
     cells = 2 * half * rows
     count, orbitals = r0.shape[0], r0.shape[2]
-    total = SLOTS * cells
     group = lax.axis_index("groups")
     z, t, c = lax.axis_index("wide"), lax.axis_index("trans"), lax.axis_index("sub")
     me = z * domains + t * sub + c
@@ -124,21 +123,37 @@
         chip, place = v // CHIP_VECTORS, v % CHIP_VECTORS
         return chip * sub + place // SLOTS, place % SLOTS
 
+    barrier = pltpu.get_barrier_semaphore()
+
+    def greet(j, carry):
+        pl.semaphore_signal(barrier, inc=1, device_id=device((me + j) % sources), device_id_type=MESH)
+        return carry
+
+    lax.fori_loop(1, sources, greet, 0)
+
+    first_load = pltpu.make_async_copy(start, raw, weight_sem.at[3])
+    region_load = pltpu.make_async_copy(region, reg_raw, weight_sem.at[4])
     loads = [
         pltpu.make_async_copy(hop, wn.at[pl.ds(0, 9)], weight_sem.at[0]),
         pltpu.make_async_copy(onsite, wn.at[pl.ds(9, 3)], weight_sem.at[1]),
         pltpu.make_async_copy(pair, wp, weight_sem.at[2]),
     ]
+    first_load.start()
+    region_load.start()
     for load in loads:
         load.start()
-
-    barrier = pltpu.get_barrier_semaphore()
-
-    def greet(j, carry):
-        pl.semaphore_signal(barrier, inc=1, device_id=device((me + j) % sources), device_id_type=MESH)
-        return carry
-
-    lax.fori_loop(1, sources, greet, 0)
+    region_load.wait()
+    lane = lax.broadcasted_iota(jnp.int32, reg.shape, 1)
+    row = jnp.zeros(reg.shape, jnp.float32)
+    for xl in range(wide_len):
+        for yl in range(row_len):
+            value = reg_raw[xl : xl + 1, yl : yl + 1].astype(jnp.float32)
+            row = jnp.where(lane == xl * row_len + yl, value, row)
+    reg[...] = row
+    first_load.wait()
+    for xl in range(wide_len):
+        wide_raw[:, xl * row_len : (xl + 1) * row_len] = raw[:, xl]
+    r0[...] = wide_raw[...].astype(jnp.bfloat16)
     pl.semaphore_wait(barrier, sources - 1)
 
     def region_copy(to, frm):
@@ -154,22 +169,28 @@
             device_id=device(to), device_id_type=MESH,
         )
 
-    def send_vector(j, carry):
-        v = (my_first + j + count // 2) % count
-
-        @pl.when(owner(v)[0] != me)
-        def _():
-            vector_copy(v, me).start()
-
-        return carry
-
-    lax.fori_loop(0, count, send_vector, 0)
+    chips = sources // sub
+
+    def send_vectors(offset):
+        def send_vector(j, carry):
+            chip = (me // sub + j + chips // 2) % chips
+            v = chip * CHIP_VECTORS + offset
+
+            @pl.when(owner(v)[0] != me)
+            def _():
+                vector_copy(v, me).start()
+
+            return carry
+
+        lax.fori_loop(0, chips, send_vector, 0)
 
     def send_region(j, carry):
         region_copy((me + j) % sources, me).start()
         return carry
 
     lax.fori_loop(1, sources, send_region, 0)
+    for offset in (0, 2, 1):
+        send_vectors(offset)
 
     regs[me] = reg[...]
     recv[0, me] = r0[my_first]
@@ -178,12 +199,7 @@
     def _():
         recv[1, me] = r0[my_first + 1]
 
-    @pl.when(c != 0)
-    def _():
-        recv[1] = jnp.zeros(recv.shape[1:], recv.dtype)
-
     buf[:, 0] = jnp.zeros((3,) + buf.shape[2:], buf.dtype)
-    previous[...] = jnp.zeros(previous.shape, jnp.float32)
     for load in loads:
         load.wait()
     for k in range(5):
@@ -196,16 +212,6 @@
     def wait_region(j, carry):
         frm = (me + j) % sources
         region_copy(frm, frm).wait_recv()
-        return carry
-
-    def wait_vector(j, carry):
-        frm = (me + j) % sources
-        for slot in range(SLOTS):
-
-            @pl.when(slot < my_slots)
-            def _():
-                vector_copy(my_first + slot, frm).wait_recv()
-
         return carry
 
     lax.fori_loop(1, sources, wait_region, 0)
@@ -218,24 +224,17 @@
     places = lax.broadcasted_iota(jnp.int32, spread.shape, 0)
     places = home_row(places, half, rows, wide_len, row_len) % per
     kinds = jnp.sum(jnp.where(lanes == places, spread, 0.0), axis=1, keepdims=True)
-    kinds = jnp.broadcast_to(kinds, (cells, orbitals)).reshape(2 * half, 1, rows, orbitals)
-    kinds = jnp.concatenate([kinds] * SLOTS, axis=1)
-    kind[...] = kinds.reshape(total, orbitals).astype(jnp.bfloat16)
-    lax.fori_loop(1, sources, wait_vector, 0)
-
-    parts = []
-    for slot in range(SLOTS):
-        part = jnp.dot(to_lattice, recv[slot].reshape(cells, orbitals), preferred_element_type=jnp.float32)
-        parts.append(part.reshape(half * 2, 1, rows, orbitals))
-    current[...] = jnp.concatenate(parts, axis=1).reshape(total, orbitals)
+    kinds = jnp.broadcast_to(kinds, (cells, orbitals))
+    for r in range(3):
+        mask[r] = jnp.where(kinds == r, 1.0, 0.0).astype(jnp.bfloat16)
 
     def store_fields():
         field = current[...]
         y = lax.broadcasted_iota(jnp.int32, field.shape, 0) % rows
         below = jnp.where(y == 0, 0.0, pltpu.roll(field, 1, 0))
-        above = jnp.where(y == rows - 1, 0.0, pltpu.roll(field, total - 1, 0))
+        above = jnp.where(y == rows - 1, 0.0, pltpu.roll(field, cells - 1, 0))
         for index, value in enumerate((below, field, above)):
-            value = value.astype(jnp.bfloat16).reshape((half, 2, SLOTS * rows, orbitals))
+            value = value.astype(jnp.bfloat16).reshape((half, 2, rows, orbitals))
             buf[index, 1 : half + 1] = value
             buf[index, half + 1, 0] = value[half - 1, 1]
             buf[index, half + 1, 1] = value[half - 1, 0]
@@ -247,71 +246,77 @@
             device_id=device(to), device_id_type=MESH,
         )
 
-    def send_home(which, values):
-        values = values.reshape(2 * half, SLOTS, rows, orbitals)
-        for slot in range(SLOTS):
-            part = lax.dot_general(
-                to_lattice, values[:, slot].reshape(cells, orbitals), (((0,), (0,)), ((), ())),
-                preferred_element_type=jnp.float32,
-            )
-            stage[which, slot] = part.astype(jnp.bfloat16).reshape(stage.shape[2:])
-
-            @pl.when(slot < my_slots)
-            def _():
-                out[which, my_first + slot] = stage[which, slot, me]
+    def send_home(which, slot, values):
+        part = lax.dot_general(
+            to_lattice, values, (((0,), (0,)), ((), ())), preferred_element_type=jnp.float32
+        )
+        stage[which, slot] = part.astype(jnp.bfloat16).reshape(stage.shape[2:])
+        out[which, my_first + slot] = stage[which, slot, me]
 
         def send(j, carry):
             to = (me + j) % sources
-            for slot in range(SLOTS):
-
-                @pl.when(slot < my_slots)
-                def _():
-                    out_copy(which, slot, to, my_first + slot).start()
-
+            out_copy(which, slot, to, my_first + slot).start()
             return carry
 
         lax.fori_loop(1, sources, send, 0)
 
     def slab(a, b):
-        return buf[b + 1, 1 + a : 1 + a + half].reshape(total, orbitals)
+        return buf[b + 1, 1 + a : 1 + a + half].reshape(cells, orbitals)
 
     def sector_slab(a, b, sector):
-        return buf[b + 1, 1 + a : 1 + a + half, sector].reshape(total // 2, orbitals)
+        return buf[b + 1, 1 + a : 1 + a + half, sector].reshape(cells // 2, orbitals)
 
     def apply(carry_scale, carry_old):
         normal = jnp.dot(slab(*HOP_OFFSETS[0]), wn[0], preferred_element_type=jnp.float32)
         for k in range(1, 9):
             normal = normal + jnp.dot(slab(*HOP_OFFSETS[k]), wn[k], preferred_element_type=jnp.float32)
         for r in range(3):
-            chosen = jnp.where(kind[...] == r, slab(0, 0), jnp.zeros((), jnp.bfloat16))
+            chosen = slab(0, 0) * mask[r]
             normal = normal + jnp.dot(chosen, wn[9 + r], preferred_element_type=jnp.float32)
-        to_e = jnp.zeros((total // 2, orbitals), jnp.float32)
-        to_h = jnp.zeros((total // 2, orbitals), jnp.float32)
+        to_e = jnp.zeros((cells // 2, orbitals), jnp.float32)
+        to_h = jnp.zeros((cells // 2, orbitals), jnp.float32)
         for k, (a, b) in enumerate(PAIR_OFFSETS):
             to_e = to_e + jnp.dot(sector_slab(a, b, 1), wp[k], preferred_element_type=jnp.float32)
             to_h = to_h + jnp.dot(sector_slab(-a, -b, 0), wpt[k], preferred_element_type=jnp.float32)
-        shape = (half, SLOTS * rows, orbitals)
-        normal = normal.reshape(half, 2, SLOTS * rows, orbitals)
+        shape = (half, rows, orbitals)
+        normal = normal.reshape(half, 2, rows, orbitals)
         new_e = normal[:, 0] + to_e.reshape(shape)
         new_h = to_h.reshape(shape) - normal[:, 1]
-        new = jnp.stack([new_e, new_h], axis=1).reshape(total, orbitals)
+        new = jnp.stack([new_e, new_h], axis=1).reshape(cells, orbitals)
         new = carry_scale * new - carry_old * previous[...]
         previous[...] = current[...]
         current[...] = new
 
-    def step(it, carry):
-        store_fields()
-
-        @pl.when(it == ITERS - 1)
+    def run(slot, carry):
+        @pl.when(slot < my_slots)
         def _():
-            send_home(1, slab(0, 0))
-
-        first = it == 0
-        apply(jnp.where(first, 1.0, 2.0), jnp.where(first, 0.0, 1.0))
-        return carry
-
-    lax.fori_loop(0, ITERS, step, 0)
-    send_home(0, current[...].astype(jnp.bfloat16))
+            def wait_vector(j, carry):
+                vector_copy(my_first + slot, (me + j) % sources).wait_recv()
+                return carry
+
+            lax.fori_loop(1, sources, wait_vector, 0)
+            current[...] = jnp.dot(
+                to_lattice, recv[slot].reshape(cells, orbitals), preferred_element_type=jnp.float32
+            )
+            previous[...] = jnp.zeros(previous.shape, jnp.float32)
+
+            def step(it, carry):
+                store_fields()
+
+                @pl.when(it == ITERS - 1)
+                def _():
+                    send_home(1, slot, slab(0, 0))
+
+                first = it == 0
+                apply(jnp.where(first, 1.0, 2.0), jnp.where(first, 0.0, 1.0))
+                return carry
+
+            lax.fori_loop(0, ITERS, step, 0)
+            send_home(0, slot, current[...].astype(jnp.bfloat16))
+
+        return carry
+
+    lax.fori_loop(0, SLOTS, run, 0)
 
     def finish_out(v, carry):
         @pl.when(owner(v)[0] != me)
@@ -346,9 +351,6 @@
     sources, per = wide * domains, wide_len * row_len
     half, rows = wide * wide_len // 2, domains * row_len
     cells = 2 * half * rows
-    total = SLOTS * cells
-    rounded = start_vectors.reshape(count, per, orbitals).astype(jnp.bfloat16)
-    regions = jnp.pad(region.reshape(1, per).astype(jnp.float32), ((0, 0), (0, 128 - per)))
     vmem = pl.BlockSpec(memory_space=pltpu.VMEM)
     hbm = pl.BlockSpec(memory_space=pl.ANY)
     bf16, f32 = jnp.bfloat16, jnp.float32
@@ -356,31 +358,36 @@
     out = pl.pallas_call(
         functools.partial(vector_kernel, sizes + (wide_len, row_len)),
         out_shape=jax.ShapeDtypeStruct((2, count, per, orbitals), bf16),
-        in_specs=[vmem, vmem, hbm, hbm, hbm],
+        in_specs=[hbm] * 5,
         out_specs=vmem,
         scratch_shapes=[
+            pltpu.VMEM(start_vectors.shape, f32),
+            pltpu.VMEM((count, per, orbitals), f32),
+            pltpu.VMEM((count, per, orbitals), bf16),
+            pltpu.VMEM(region.shape, region.dtype),
+            pltpu.VMEM((1, 128), f32),
             pltpu.VMEM((SLOTS, sources, per, orbitals), bf16),
             pltpu.VMEM((sources, 1, 128), f32),
             pltpu.VMEM((12, orbitals, orbitals), bf16),
             pltpu.VMEM((5, orbitals, orbitals), bf16),
             pltpu.VMEM((5, orbitals, orbitals), bf16),
-            pltpu.VMEM((3, half + 2, 2, SLOTS * rows, orbitals), bf16),
-            pltpu.VMEM((total, orbitals), f32),
-            pltpu.VMEM((total, orbitals), f32),
+            pltpu.VMEM((3, half + 2, 2, rows, orbitals), bf16),
+            pltpu.VMEM((cells, orbitals), f32),
+            pltpu.VMEM((cells, orbitals), f32),
             pltpu.VMEM((2, SLOTS, sources, per, orbitals), bf16),
-            pltpu.VMEM((total, orbitals), bf16),
+            pltpu.VMEM((3, cells, orbitals), bf16),
             dma((count,)),
             dma((SLOTS, sources)),
             dma((sources,)),
             dma((sources,)),
             dma((2, SLOTS, sources)),
             dma((2, count)),
-            dma((3,)),
+            dma((5,)),
         ],
         compiler_params=pltpu.CompilerParams(
-            collective_id=0, has_side_effects=True, vmem_limit_bytes=40 * 2**20
+            collective_id=0, has_side_effects=True, vmem_limit_bytes=60 * 2**20
         ),
-    )(rounded, regions, hopping, pairing, onsite)
+    )(start_vectors, region, hopping, pairing, onsite)
     wanted = out.astype(f32).reshape((2,) + start_vectors.shape)
     return wanted[0], wanted[1]
 

time: 38.5 us -> 31 us (0.81)
  Pallas kernels: 31.6 us -> 27.4 us
  other arithmetic: 1.82 us -> 0 us
  local copies, waits for them, and re-layouts: 4.22 us -> 2.83 us
    pallas_call x1, Pallas kernels: 31.6 us -> 27.4 us  [by_vectors(): pl.pallas_call(functools.partial(vector_kernel, sizes + (wide_len, row_le...]
    unnamed x6 -> x0, local copies, waits for them, and re-layouts: 2.27 us -> none
    convert_element_type x2 -> x0, other arithmetic: 1.82 us -> none  [the longest x1 1.07 us: by_vectors(): rounded = start_vectors.reshape(count, per, orbitals).astype(jnp.bfloat16)]
    slice x1, local copies, waits for them, and re-layouts: 0.09 us -> 1.11 us  [by_vectors(): return (wanted[0], wanted[1])]
where the time goes in v2:
time: 31 us; the launch traced here: 30.9 us
  Pallas kernels  27.4 us (88%)
  local copies, waits for them, and re-layouts  2.83 us (9%)
  between operations  0.65 us (2%)
    pallas_call x1, Pallas kernels, by_vectors(): pl.pallas_call(functools.partial(vector_kernel, sizes + (wide_len, row_le...  27.4 us
    squeeze x2, local copies, waits for them, and re-layouts, by_vectors(): return (wanted[0], wanted[1])  1.72 us
    slice x1, local copies, waits for them, and re-layouts, by_vectors(): return (wanted[0], wanted[1])  1.11 us

profile of v2, /device:TPU:0, one launch (start us, length us, event | category | flops | bytes accessed | tf_op | source)
XLA Modules:
  0.0 30.9 jit_solution(16125564139573680764)
XLA Ops:
  0.6 27.4 %shard_map.68 = bf16[2,24,16,256]{3,2,1,0:T(8,128)(2,1)} custom-call(f32[24,4,4,256]{3,2,1,0:T(4,128)} %start.1, s32[4,4]{1,0:T(4,128)} %region.1, bf16[9,256,256]{2,1,0:T(8,128)(2,1)} %hop.1, bf16[5,256,256]{2,1,0:T(8,128)(2,1)} %pair.1, bf16[3,256,256]{2,1,0:T(8,128)(2,1)} %onsite.1), custom_call_target="tpu_custom_call" | custom-call | tf_op jit(solution)/shard_map/pallas_call | solution.py:358
  28.1 1.1 %fusion = (f32[1,24,16,256]{3,2,1,0:T(8,128)S(1)}, f32[1,24,16,256]{3,2,1,0:T(8,128)S(1)}) fusion(bf16[2,24,16,256]{3,2,1,0:T(8,128)(2,1)} %shard_map.68), kind=kLoop, calls=%fused_computation | loop fusion | bytes 1572864 | tf_op jit(solution)/shard_map/slice | solution.py:392
  29.2 0.9 %squeeze.7 = f32[24,4,4,256]{3,2,1,0:T(4,128)} reshape(f32[1,24,16,256]{3,2,1,0:T(8,128)S(1)} %get-tuple-element.2) | data formatting | bytes 786432 | tf_op jit(solution)/shard_map/squeeze | solution.py:392
  30.0 0.9 %squeeze.6 = f32[24,4,4,256]{3,2,1,0:T(4,128)} reshape(f32[1,24,16,256]{3,2,1,0:T(8,128)S(1)} %get-tuple-element.3) | data formatting | bytes 786432 | tf_op jit(solution)/shard_map/squeeze | solution.py:392

commit v3 on v2

--- a/solution.py
+++ b/solution.py
@@ -99,8 +99,8 @@
 
 
 def vector_kernel(
-    sizes, start, region, hop, pair, onsite, out,
-    raw, wide_raw, r0, reg_raw, reg, recv, regs, wn, wp, wpt, buf, previous, current, stage, mask,
+    sizes, start, region, hop, pair, onsite, last, before,
+    raw, wide_raw, out, r0, reg_raw, reg, recv, regs, wn, wp, wpt, buf, previous, current, stage, mask,
     send_sem, recv_sem, rsend_sem, rrecv_sem, osend_sem, orecv_sem, weight_sem,
 ):
     wide, trans, sub, wide_len, row_len = sizes
@@ -116,22 +116,20 @@
     my_first = (z * trans + t) * CHIP_VECTORS + c * SLOTS
     my_slots = SLOTS - c
 
-    def device(index):
-        return (group, index // domains, (index % domains) // sub, index % sub)
-
-    def owner(v):
-        chip, place = v // CHIP_VECTORS, v % CHIP_VECTORS
-        return chip * sub + place // SLOTS, place % SLOTS
+    peers = []
+    for dz in sorted(range(wide), key=lambda dz: -min(dz, wide - dz)):
+        for dt in range(trans):
+            for dc in range(sub):
+                if dz or dt or dc:
+                    to_z, to_t, to_c = lax.rem(z + dz, wide), lax.rem(t + dt, trans), lax.rem(c + dc, sub)
+                    peers.append(((group, to_z, to_t, to_c), to_z * domains + to_t * sub + to_c))
 
     barrier = pltpu.get_barrier_semaphore()
 
-    def greet(j, carry):
-        pl.semaphore_signal(barrier, inc=1, device_id=device((me + j) % sources), device_id_type=MESH)
-        return carry
-
-    lax.fori_loop(1, sources, greet, 0)
-
-    first_load = pltpu.make_async_copy(start, raw, weight_sem.at[3])
+    for place, index in peers:
+        pl.semaphore_signal(barrier, inc=1, device_id=place, device_id_type=MESH)
+
+    first_load = pltpu.make_async_copy(start, raw.at[0], weight_sem.at[3])
     region_load = pltpu.make_async_copy(region, reg_raw, weight_sem.at[4])
     loads = [
         pltpu.make_async_copy(hop, wn.at[pl.ds(0, 9)], weight_sem.at[0]),
@@ -152,45 +150,30 @@
     reg[...] = row
     first_load.wait()
     for xl in range(wide_len):
-        wide_raw[:, xl * row_len : (xl + 1) * row_len] = raw[:, xl]
+        wide_raw[:, xl * row_len : (xl + 1) * row_len] = raw[0, :, xl]
     r0[...] = wide_raw[...].astype(jnp.bfloat16)
     pl.semaphore_wait(barrier, sources - 1)
 
-    def region_copy(to, frm):
-        return pltpu.make_async_remote_copy(
-            src_ref=reg, dst_ref=regs.at[frm], send_sem=rsend_sem.at[to], recv_sem=rrecv_sem.at[frm],
-            device_id=device(to), device_id_type=MESH,
-        )
-
-    def vector_copy(v, frm):
-        to, slot = owner(v)
-        return pltpu.make_async_remote_copy(
-            src_ref=r0.at[v], dst_ref=recv.at[slot, frm], send_sem=send_sem.at[v], recv_sem=recv_sem.at[slot, frm],
-            device_id=device(to), device_id_type=MESH,
-        )
-
-    chips = sources // sub
-
-    def send_vectors(offset):
-        def send_vector(j, carry):
-            chip = (me // sub + j + chips // 2) % chips
-            v = chip * CHIP_VECTORS + offset
-
-            @pl.when(owner(v)[0] != me)
-            def _():
-                vector_copy(v, me).start()
-
-            return carry
-
-        lax.fori_loop(0, chips, send_vector, 0)
-
-    def send_region(j, carry):
-        region_copy((me + j) % sources, me).start()
-        return carry
-
-    lax.fori_loop(1, sources, send_region, 0)
+    for place, index in peers:
+        pltpu.make_async_remote_copy(
+            src_ref=reg, dst_ref=regs.at[me], send_sem=rsend_sem.at[0], recv_sem=rrecv_sem.at[0],
+            device_id=place, device_id_type=MESH,
+        ).start()
+
     for offset in (0, 2, 1):
-        send_vectors(offset)
+        core, slot = offset // SLOTS, offset % SLOTS
+        for dz in sorted(range(wide), key=lambda dz: -min(dz, wide - dz)):
+            for dt in range(trans):
+                to_z, to_t = lax.rem(z + dz, wide), lax.rem(t + dt, trans)
+                v = (to_z * trans + to_t) * CHIP_VECTORS + offset
+                copy = pltpu.make_async_remote_copy(
+                    src_ref=r0.at[v], dst_ref=recv.at[slot, me], send_sem=send_sem.at[0], recv_sem=recv_sem.at[slot],
+                    device_id=(group, to_z, to_t, jnp.int32(core)), device_id_type=MESH,
+                )
+                if dz or dt:
+                    copy.start()
+                else:
+                    pl.when(c != core)(copy.start)
 
     regs[me] = reg[...]
     recv[0, me] = r0[my_first]
@@ -209,12 +192,12 @@
     home = lax.broadcasted_iota(jnp.int32, (cells, cells), 1)
     to_lattice = (home_row(lattice, half, rows, wide_len, row_len) == home).astype(jnp.bfloat16)
 
-    def wait_region(j, carry):
-        frm = (me + j) % sources
-        region_copy(frm, frm).wait_recv()
-        return carry
-
-    lax.fori_loop(1, sources, wait_region, 0)
+    others = sources - 1
+
+    def arrived(ref, sem):
+        pltpu.make_async_copy(ref, ref, sem).wait()
+
+    arrived(regs.at[pl.ds(0, others)], rrecv_sem.at[0])
     per = wide_len * row_len
     spots = lax.broadcasted_iota(jnp.int32, (cells, sources), 0)
     spots = home_row(spots, half, rows, wide_len, row_len)
@@ -239,13 +222,6 @@
             buf[index, half + 1, 0] = value[half - 1, 1]
             buf[index, half + 1, 1] = value[half - 1, 0]
 
-    def out_copy(which, slot, to, v):
-        return pltpu.make_async_remote_copy(
-            src_ref=stage.at[which, slot, to], dst_ref=out.at[which, v],
-            send_sem=osend_sem.at[which, slot, to], recv_sem=orecv_sem.at[which, v],
-            device_id=device(to), device_id_type=MESH,
-        )
-
     def send_home(which, slot, values):
         part = lax.dot_general(
             to_lattice, values, (((0,), (0,)), ((), ())), preferred_element_type=jnp.float32
@@ -253,12 +229,12 @@
         stage[which, slot] = part.astype(jnp.bfloat16).reshape(stage.shape[2:])
         out[which, my_first + slot] = stage[which, slot, me]
 
-        def send(j, carry):
-            to = (me + j) % sources
-            out_copy(which, slot, to, my_first + slot).start()
-            return carry
-
-        lax.fori_loop(1, sources, send, 0)
+        for place, index in peers:
+            pltpu.make_async_remote_copy(
+                src_ref=stage.at[which, slot, index], dst_ref=out.at[which, my_first + slot],
+                send_sem=osend_sem.at[which, slot], recv_sem=orecv_sem.at[which],
+                device_id=place, device_id_type=MESH,
+            ).start()
 
     def slab(a, b):
         return buf[b + 1, 1 + a : 1 + a + half].reshape(cells, orbitals)
@@ -290,11 +266,7 @@
     def run(slot, carry):
         @pl.when(slot < my_slots)
         def _():
-            def wait_vector(j, carry):
-                vector_copy(my_first + slot, (me + j) % sources).wait_recv()
-                return carry
-
-            lax.fori_loop(1, sources, wait_vector, 0)
+            arrived(recv.at[slot, pl.ds(0, others)], recv_sem.at[slot])
             current[...] = jnp.dot(
                 to_lattice, recv[slot].reshape(cells, orbitals), preferred_element_type=jnp.float32
             )
@@ -318,30 +290,34 @@
 
     lax.fori_loop(0, SLOTS, run, 0)
 
-    def finish_out(v, carry):
-        @pl.when(owner(v)[0] != me)
+    for which, result in ((1, before), (0, last)):
+        for core in range(sub):
+
+            @pl.when(c == core)
+            def _():
+                arrived(out.at[which, pl.ds(0, count - SLOTS + core)], orecv_sem.at[which])
+
+        wide_raw[...] = out[which].astype(jnp.float32)
+        for xl in range(wide_len):
+            raw[which, :, xl] = wide_raw[:, xl * row_len : (xl + 1) * row_len]
+        pltpu.make_async_copy(raw.at[which], result, weight_sem.at[which]).start()
+
+    for core in range(sub):
+
+        @pl.when(c == core)
         def _():
-            vector_copy(v, me).wait_send()
+            arrived(r0.at[pl.ds(0, count - SLOTS + core)], send_sem.at[0])
+
+    arrived(regs.at[pl.ds(0, others)], rsend_sem.at[0])
+    for slot in range(SLOTS):
+
+        @pl.when(slot < my_slots)
+        def _():
             for which in range(2):
-                out_copy(which, 0, owner(v)[0], v).wait_recv()
-
-        return carry
-
-    lax.fori_loop(0, count, finish_out, 0)
-
-    def finish_sends(j, carry):
-        to = (me + j) % sources
-        region_copy(to, me).wait_send()
-        for slot in range(SLOTS):
-
-            @pl.when(slot < my_slots)
-            def _():
-                for which in range(2):
-                    out_copy(which, slot, to, my_first + slot).wait_send()
-
-        return carry
-
-    lax.fori_loop(1, sources, finish_sends, 0)
+                arrived(stage.at[which, slot, pl.ds(0, others)], osend_sem.at[which, slot])
+
+    for which, result in ((1, before), (0, last)):
+        pltpu.make_async_copy(raw.at[which], result, weight_sem.at[which]).wait()
 
 
 def by_vectors(sizes, start_vectors, hopping, pairing, onsite, region):
@@ -351,18 +327,18 @@
     sources, per = wide * domains, wide_len * row_len
     half, rows = wide * wide_len // 2, domains * row_len
     cells = 2 * half * rows
-    vmem = pl.BlockSpec(memory_space=pltpu.VMEM)
     hbm = pl.BlockSpec(memory_space=pl.ANY)
     bf16, f32 = jnp.bfloat16, jnp.float32
     dma = pltpu.SemaphoreType.DMA
-    out = pl.pallas_call(
+    return pl.pallas_call(
         functools.partial(vector_kernel, sizes + (wide_len, row_len)),
-        out_shape=jax.ShapeDtypeStruct((2, count, per, orbitals), bf16),
+        out_shape=(jax.ShapeDtypeStruct(start_vectors.shape, f32),) * 2,
         in_specs=[hbm] * 5,
-        out_specs=vmem,
+        out_specs=(hbm, hbm),
         scratch_shapes=[
-            pltpu.VMEM(start_vectors.shape, f32),
+            pltpu.VMEM((2,) + start_vectors.shape, f32),
             pltpu.VMEM((count, per, orbitals), f32),
+            pltpu.VMEM((2, count, per, orbitals), bf16),
             pltpu.VMEM((count, per, orbitals), bf16),
             pltpu.VMEM(region.shape, region.dtype),
             pltpu.VMEM((1, 128), f32),
@@ -376,20 +352,18 @@
             pltpu.VMEM((cells, orbitals), f32),
             pltpu.VMEM((2, SLOTS, sources, per, orbitals), bf16),
             pltpu.VMEM((3, cells, orbitals), bf16),
-            dma((count,)),
-            dma((SLOTS, sources)),
-            dma((sources,)),
-            dma((sources,)),
-            dma((2, SLOTS, sources)),
-            dma((2, count)),
+            dma((1,)),
+            dma((SLOTS,)),
+            dma((1,)),
+            dma((1,)),
+            dma((2, SLOTS)),
+            dma((2,)),
             dma((5,)),
         ],
         compiler_params=pltpu.CompilerParams(
             collective_id=0, has_side_effects=True, vmem_limit_bytes=60 * 2**20
         ),
     )(start_vectors, region, hopping, pairing, onsite)
-    wanted = out.astype(f32).reshape((2,) + start_vectors.shape)
-    return wanted[0], wanted[1]
 
 
 def solution(mesh):

time: 31 us -> 29.9 us (0.965)
  Pallas kernels: 27.4 us -> 25.5 us
  local copies, waits for them, and re-layouts: 2.83 us -> 3.53 us
    unnamed x0 -> x2, local copies, waits for them, and re-layouts: none -> 3.53 us
    pallas_call x1, Pallas kernels: 27.4 us -> 25.5 us  [by_vectors(): pl.pallas_call(functools.partial(vector_kernel, sizes + (wide_len, row_le...]
    squeeze x2 -> x0, local copies, waits for them, and re-layouts: 1.72 us -> none  [by_vectors(): return (wanted[0], wanted[1])]
    slice x1 -> x0, local copies, waits for them, and re-layouts: 1.11 us -> none  [by_vectors(): return (wanted[0], wanted[1])]
where the time goes in v3:
time: 29.9 us; the launch traced here: 29.7 us
  Pallas kernels  25.5 us (85%)
  local copies, waits for them, and re-layouts  3.53 us (12%)
  between operations  0.64 us (2%)
    pallas_call x1, Pallas kernels, by_vectors(): pl.pallas_call(functools.partial(vector_kernel, sizes + (wide_len, row_le...  25.5 us
    unnamed x2, local copies, waits for them, and re-layouts  3.53 us

profile of v3, /device:TPU:0, one launch (start us, length us, event | category | flops | bytes accessed | tf_op | source)
XLA Modules:
  0.0 29.7 jit_solution(1213957788769867638)
XLA Ops:
  0.6 25.5 %shard_map.68 = (f32[24,4,4,256]{3,2,1,0:T(4,128)}, f32[24,4,4,256]{3,2,1,0:T(4,128)}) custom-call(f32[24,4,4,256]{3,2,1,0:T(4,128)} %start.1, s32[4,4]{1,0:T(4,128)} %region.1, bf16[9,256,256]{2,1,0:T(8,128)(2,1)} %hop.1, bf16[5,256,256]{2,1,0:T(8,128)(2,1)} %pair.1, bf16[3,256,256]{2,1,0:T(8,128)(2,1)} %onsite.1), custom_call_target="tpu_custom_call" | custom-call | tf_op jit(solution)/shard_map/pallas_call | solution.py:333
  26.1 1.8 %copy.9 = f32[24,4,4,256]{3,2,1,0:T(4,128)} copy(f32[24,4,4,256]{3,2,1,0:T(4,128)} %get-tuple-element.4) | data formatting | bytes 786432
  27.9 1.8 %copy.10 = f32[24,4,4,256]{3,2,1,0:T(4,128)} copy(f32[24,4,4,256]{3,2,1,0:T(4,128)} %get-tuple-element.5) | data formatting | bytes 786432

commit v4 on v3

--- a/solution.py
+++ b/solution.py
@@ -99,8 +99,8 @@
 
 
 def vector_kernel(
-    sizes, start, region, hop, pair, onsite, last, before,
-    raw, wide_raw, out, r0, reg_raw, reg, recv, regs, wn, wp, wpt, buf, previous, current, stage, mask,
+    sizes, start, region, hop, pair, onsite, results,
+    raw, wide_raw, final, out, r0, reg_raw, reg, recv, regs, wn, wp, wpt, buf, previous, current, stage, mask,
     send_sem, recv_sem, rsend_sem, rrecv_sem, osend_sem, orecv_sem, weight_sem,
 ):
     wide, trans, sub, wide_len, row_len = sizes
@@ -129,7 +129,7 @@
     for place, index in peers:
         pl.semaphore_signal(barrier, inc=1, device_id=place, device_id_type=MESH)
 
-    first_load = pltpu.make_async_copy(start, raw.at[0], weight_sem.at[3])
+    first_load = pltpu.make_async_copy(start, raw, weight_sem.at[3])
     region_load = pltpu.make_async_copy(region, reg_raw, weight_sem.at[4])
     loads = [
         pltpu.make_async_copy(hop, wn.at[pl.ds(0, 9)], weight_sem.at[0]),
@@ -150,7 +150,7 @@
     reg[...] = row
     first_load.wait()
     for xl in range(wide_len):
-        wide_raw[:, xl * row_len : (xl + 1) * row_len] = raw[0, :, xl]
+        wide_raw[:, xl * row_len : (xl + 1) * row_len] = raw[:, xl]
     r0[...] = wide_raw[...].astype(jnp.bfloat16)
     pl.semaphore_wait(barrier, sources - 1)
 
@@ -243,17 +243,19 @@
         return buf[b + 1, 1 + a : 1 + a + half, sector].reshape(cells // 2, orbitals)
 
     def apply(carry_scale, carry_old):
-        normal = jnp.dot(slab(*HOP_OFFSETS[0]), wn[0], preferred_element_type=jnp.float32)
-        for k in range(1, 9):
-            normal = normal + jnp.dot(slab(*HOP_OFFSETS[k]), wn[k], preferred_element_type=jnp.float32)
-        for r in range(3):
-            chosen = slab(0, 0) * mask[r]
-            normal = normal + jnp.dot(chosen, wn[9 + r], preferred_element_type=jnp.float32)
-        to_e = jnp.zeros((cells // 2, orbitals), jnp.float32)
-        to_h = jnp.zeros((cells // 2, orbitals), jnp.float32)
-        for k, (a, b) in enumerate(PAIR_OFFSETS):
-            to_e = to_e + jnp.dot(sector_slab(a, b, 1), wp[k], preferred_element_type=jnp.float32)
-            to_h = to_h + jnp.dot(sector_slab(-a, -b, 0), wpt[k], preferred_element_type=jnp.float32)
+        normal_slabs = [slab(a, b) for a, b in HOP_OFFSETS] + [slab(0, 0) * mask[r] for r in range(3)]
+        normal = jnp.dot(
+            jnp.concatenate(normal_slabs, axis=1), wn[...].reshape(12 * orbitals, orbitals),
+            preferred_element_type=jnp.float32,
+        )
+        to_e = jnp.dot(
+            jnp.concatenate([sector_slab(a, b, 1) for a, b in PAIR_OFFSETS], axis=1),
+            wp[...].reshape(5 * orbitals, orbitals), preferred_element_type=jnp.float32,
+        )
+        to_h = jnp.dot(
+            jnp.concatenate([sector_slab(-a, -b, 0) for a, b in PAIR_OFFSETS], axis=1),
+            wpt[...].reshape(5 * orbitals, orbitals), preferred_element_type=jnp.float32,
+        )
         shape = (half, rows, orbitals)
         normal = normal.reshape(half, 2, rows, orbitals)
         new_e = normal[:, 0] + to_e.reshape(shape)
@@ -290,7 +292,7 @@
 
     lax.fori_loop(0, SLOTS, run, 0)
 
-    for which, result in ((1, before), (0, last)):
+    for which in (1, 0):
         for core in range(sub):
 
             @pl.when(c == core)
@@ -299,8 +301,8 @@
 
         wide_raw[...] = out[which].astype(jnp.float32)
         for xl in range(wide_len):
-            raw[which, :, xl] = wide_raw[:, xl * row_len : (xl + 1) * row_len]
-        pltpu.make_async_copy(raw.at[which], result, weight_sem.at[which]).start()
+            final[which, :, xl] = wide_raw[:, xl * row_len : (xl + 1) * row_len].astype(jnp.bfloat16)
+        pltpu.make_async_copy(final.at[which], results.at[which], weight_sem.at[which]).start()
 
     for core in range(sub):
 
@@ -316,8 +318,8 @@
             for which in range(2):
                 arrived(stage.at[which, slot, pl.ds(0, others)], osend_sem.at[which, slot])
 
-    for which, result in ((1, before), (0, last)):
-        pltpu.make_async_copy(raw.at[which], result, weight_sem.at[which]).wait()
+    for which in (1, 0):
+        pltpu.make_async_copy(final.at[which], results.at[which], weight_sem.at[which]).wait()
 
 
 def by_vectors(sizes, start_vectors, hopping, pairing, onsite, region):
@@ -330,14 +332,15 @@
     hbm = pl.BlockSpec(memory_space=pl.ANY)
     bf16, f32 = jnp.bfloat16, jnp.float32
     dma = pltpu.SemaphoreType.DMA
-    return pl.pallas_call(
+    results = pl.pallas_call(
         functools.partial(vector_kernel, sizes + (wide_len, row_len)),
-        out_shape=(jax.ShapeDtypeStruct(start_vectors.shape, f32),) * 2,
+        out_shape=jax.ShapeDtypeStruct((2,) + start_vectors.shape, bf16),
         in_specs=[hbm] * 5,
-        out_specs=(hbm, hbm),
+        out_specs=hbm,
         scratch_shapes=[
-            pltpu.VMEM((2,) + start_vectors.shape, f32),
+            pltpu.VMEM(start_vectors.shape, f32),
             pltpu.VMEM((count, per, orbitals), f32),
+            pltpu.VMEM((2,) + start_vectors.shape, bf16),
             pltpu.VMEM((2, count, per, orbitals), bf16),
             pltpu.VMEM((count, per, orbitals), bf16),
             pltpu.VMEM(region.shape, region.dtype),
@@ -364,6 +367,7 @@
             collective_id=0, has_side_effects=True, vmem_limit_bytes=60 * 2**20
         ),
     )(start_vectors, region, hopping, pairing, onsite)
+    return results[0].astype(f32), results[1].astype(f32)
 
 
 def solution(mesh):

time: 29.9 us -> 28.4 us (0.950)
  local copies, waits for them, and re-layouts: 3.53 us -> 0 us
  other arithmetic: 0 us -> 2.13 us
    unnamed x2 -> x0, local copies, waits for them, and re-layouts: 3.53 us -> none
    convert_element_type x0 -> x1, other arithmetic: none -> 2.13 us  [by_vectors(): return (results[0].astype(f32), results[1].astype(f32))]
where the time goes in v4:
time: 28.4 us; the launch traced here: 28.2 us
  Pallas kernels  25.4 us (89%)
  other arithmetic  2.13 us (8%)
  between operations  0.64 us (2%)
    pallas_call x1, Pallas kernels, by_vectors(): pl.pallas_call(functools.partial(vector_kernel, sizes + (wide_len, row_le...  25.4 us
    convert_element_type x1, other arithmetic, by_vectors(): return (results[0].astype(f32), results[1].astype(f32))  2.13 us

profile of v4, /device:TPU:0, one launch (start us, length us, event | category | flops | bytes accessed | tf_op | source)
XLA Modules:
  0.0 28.2 jit_solution(14149175155278255298)
XLA Ops:
  0.6 25.4 %shard_map.68 = bf16[2,24,4,4,256]{4,3,2,1,0:T(4,128)(2,1)} custom-call(f32[24,4,4,256]{3,2,1,0:T(4,128)} %start.1, s32[4,4]{1,0:T(4,128)} %region.1, bf16[9,256,256]{2,1,0:T(8,128)(2,1)} %hop.1, bf16[5,256,256]{2,1,0:T(8,128)(2,1)} %pair.1, bf16[3,256,256]{2,1,0:T(8,128)(2,1)} %onsite.1), custom_call_target="tpu_custom_call" | custom-call | tf_op jit(solution)/shard_map/pallas_call | solution.py:335
  26.1 2.1 %bitcast_convert_fusion = (f32[24,4,4,256]{3,2,1,0:T(4,128)}, f32[24,4,4,256]{3,2,1,0:T(4,128)}) fusion(bf16[2,24,4,4,256]{4,3,2,1,0:T(4,128)(2,1)} %shard_map.68), kind=kLoop, calls=%fused_computation | loop fusion | flops 196608 | bytes 1179648 | tf_op jit(solution)/shard_map/convert_element_type | solution.py:370

commit v5 on v4

--- a/solution.py
+++ b/solution.py
@@ -299,9 +299,9 @@
             def _():
                 arrived(out.at[which, pl.ds(0, count - SLOTS + core)], orecv_sem.at[which])
 
-        wide_raw[...] = out[which].astype(jnp.float32)
+        arrivals = out[which].astype(jnp.float32)
         for xl in range(wide_len):
-            final[which, :, xl] = wide_raw[:, xl * row_len : (xl + 1) * row_len].astype(jnp.bfloat16)
+            final[which, :, xl] = arrivals[:, xl * row_len : (xl + 1) * row_len].astype(jnp.bfloat16)
         pltpu.make_async_copy(final.at[which], results.at[which], weight_sem.at[which]).start()
 
     for core in range(sub):

time: 28.4 us -> 28.3 us (level)
  no operation moved by 1% of the time
where the time goes in v5:
time: 28.3 us; the launch traced here: 28.2 us
  Pallas kernels  25.4 us (90%)
  other arithmetic  2.13 us (8%)
  between operations  0.64 us (2%)
    pallas_call x1, Pallas kernels, by_vectors(): pl.pallas_call(functools.partial(vector_kernel, sizes + (wide_len, row_le...  25.4 us
    convert_element_type x1, other arithmetic, by_vectors(): return (results[0].astype(f32), results[1].astype(f32))  2.13 us

profile of v5, /device:TPU:0, one launch (start us, length us, event | category | flops | bytes accessed | tf_op | source)
XLA Modules:
  0.0 28.2 jit_solution(5824564743777394332)
XLA Ops:
  0.6 25.4 %shard_map.68 = bf16[2,24,4,4,256]{4,3,2,1,0:T(4,128)(2,1)} custom-call(f32[24,4,4,256]{3,2,1,0:T(4,128)} %start.1, s32[4,4]{1,0:T(4,128)} %region.1, bf16[9,256,256]{2,1,0:T(8,128)(2,1)} %hop.1, bf16[5,256,256]{2,1,0:T(8,128)(2,1)} %pair.1, bf16[3,256,256]{2,1,0:T(8,128)(2,1)} %onsite.1), custom_call_target="tpu_custom_call" | custom-call | tf_op jit(solution)/shard_map/pallas_call | solution.py:335
  26.0 2.1 %bitcast_convert_fusion = (f32[24,4,4,256]{3,2,1,0:T(4,128)}, f32[24,4,4,256]{3,2,1,0:T(4,128)}) fusion(bf16[2,24,4,4,256]{4,3,2,1,0:T(4,128)(2,1)} %shard_map.68), kind=kLoop, calls=%fused_computation | loop fusion | flops 196608 | bytes 1179648 | tf_op jit(solution)/shard_map/convert_element_type | solution.py:370
